TPU v7x, 256 devices: a whole 4x4x8 slice. The times are simulated.
256 devices in a mesh: dp: 32 (over y_hi, z, core), blk: 8 (over x, y_lo).
Axes of the slice: x: 4, y: 4 (y_hi: 2, y_lo: 2; y = y_hi * 2 + y_lo), z: 8, core: 2. Of those that a mesh axis runs over, the one named last changes fastest.
Arguments:
- patches: bfloat16 [32, 8, 256, 1152], P('dp', 'blk'), may hold values from -8 to 8
- counts: int32 [32, 8, 1], P('dp', 'blk'), may hold values from 1 to 256, as said below
- norm_gain: float32 [1152], replicated, may hold values from 0.1 to 1.9
- norm_bias: float32 [1152], replicated, may hold values from -3 to 3
- weight_in: bfloat16 [1152, 4304], P('dp'), may hold values from -0.1875 to 0.1875
- bias_in: float32 [4304], replicated, may hold values from -3 to 3
- weight_out: bfloat16 [4304, 1152], P(None, 'dp'), may hold values from -0.09375 to 0.09375
- bias_out: float32 [1152], replicated, may hold values from -3 to 3
- text_embed: bfloat16 [256, 1152], P(('dp', 'blk')), may hold values from -0.19921875 to 0.19921875
- pair_label: int32 [256], replicated, may hold values from 0 to 63
- logit_params: float32 [2], replicated, may hold values from -5 to 2.5, as said below
Outputs:
- patch_grad: bfloat16 [32, 8, 256, 1152], P('dp', 'blk')
- text_grad: bfloat16 [256, 1152], P(('dp', 'blk'))
- statistics: float32 [3], replicated
Inputs may be any that keep to these rules, and one draw needn't show every extreme that they name: `counts`: the count of each device is 8 times a whole number from 1 to 32; over the devices of one blk index they sum to 4096; on one device of each blk index every count is 256. `logit_params`: the first entry is the logarithm of the logit scale, the second the logit bias.
All inputs are finite; a program needn't handle non-finite values.
Results may differ from a plain program's by a relative error of at most 0.0056.
Values may be sent and summed in bfloat16 or wider, within the bound.
A program may use at most 128 MiB of HBM per device.

v0:
```python
import jax
import jax.numpy as jnp
from jax import lax
from jax.sharding import PartitionSpec as P

ROWS_DEV = 128


NORM_EPS = 1e-06
GELU_SCALE = 0.7978845608028654
GELU_CUBIC = 0.044715


def from_behind(value, axis, steps):
    count = lax.axis_size(axis)
    pairs = [(source, (source + steps) % count) for source in range(count)]
    return lax.ppermute(value, axis, pairs)


def gelu_parts(pre_act):
    inner = GELU_SCALE * (pre_act + GELU_CUBIC * pre_act * pre_act * pre_act)
    tanh_vals = jnp.tanh(inner)
    value = 0.5 * pre_act * (1.0 + tanh_vals)
    slope = 0.5 * (1.0 + tanh_vals) + 0.5 * pre_act * (1.0 - tanh_vals * tanh_vals) * GELU_SCALE * (
        1.0 + 3.0 * GELU_CUBIC * pre_act * pre_act
    )
    return (value, slope)


def layer_norm(rows, norm_gain, norm_bias):
    wide_rows = rows.astype(jnp.float32)
    centre = wide_rows - jnp.mean(wide_rows, axis=-1, keepdims=True)
    inv_std = lax.rsqrt(jnp.mean(centre * centre, axis=-1, keepdims=True) + NORM_EPS)
    plain_rows = centre * inv_std
    return (plain_rows, inv_std, (plain_rows * norm_gain + norm_bias).astype(jnp.bfloat16))


def contract_last(left, right):
    return lax.dot_general(
        left, right, (((1,), (1,)), ((), ())), preferred_element_type=jnp.float32
    )


def forward_rows(rows, params, whole_weights):
    norm_gain, norm_bias, weight_in, bias_in, weight_out, bias_out = params
    plain_rows, inv_std, normed = layer_norm(rows, norm_gain, norm_bias)
    pre_act = jnp.dot(normed, whole_weights[0], preferred_element_type=jnp.float32)
    hidden, gelu_slope = gelu_parts(pre_act + bias_in)
    hidden_bf = hidden.astype(jnp.bfloat16)
    mixed = jnp.dot(hidden_bf, whole_weights[1], preferred_element_type=jnp.float32)
    out_rows = rows.astype(jnp.float32) + mixed + bias_out
    return (out_rows, (plain_rows, inv_std, gelu_slope))


def backward_rows(row_grad, saved_parts, params, whole_weights):
    norm_gain, norm_bias, weight_in, bias_in, weight_out, bias_out = params
    plain_rows, inv_std, gelu_slope = saved_parts
    grad_bf = row_grad.astype(jnp.bfloat16)
    act_grad = contract_last(grad_bf, whole_weights[1])
    pre_grad = (act_grad * gelu_slope).astype(jnp.bfloat16)
    normed_grad = contract_last(pre_grad, whole_weights[0])
    plain_grad = normed_grad * norm_gain
    input_grad = inv_std * (
        plain_grad
        - jnp.mean(plain_grad, axis=-1, keepdims=True)
        - plain_rows * jnp.mean(plain_grad * plain_rows, axis=-1, keepdims=True)
    )
    return row_grad + input_grad


def shards(
    patches,
    counts,
    norm_gain,
    norm_bias,
    weight_in,
    bias_in,
    weight_out,
    bias_out,
    text_embed,
    pair_label,
    logit_params,
):
    feat_width = patches.shape[3]
    rows_pad = patches.shape[2]
    image_count = counts.shape[2]
    patch_max = rows_pad // image_count
    dp_count = lax.axis_size("dp")
    blk_count = lax.axis_size("blk")
    my_rank = lax.axis_index("dp")
    my_blk = lax.axis_index("blk")
    flat_rows = patches.reshape(rows_pad, feat_width)
    own_counts = counts.reshape(image_count)
    count_f = own_counts.astype(jnp.float32)
    image_ids = jnp.arange(image_count, dtype=jnp.int32)
    params = (norm_gain, norm_bias, weight_in, bias_in, weight_out, bias_out)
    whole_weights = None
    whole_weights = (
        lax.all_gather(weight_in, "dp", axis=0, tiled=True),
        lax.all_gather(weight_out, "dp", axis=1, tiled=True),
    )
    slot_cap = 2 * ROWS_DEV // dp_count
    half_count = dp_count // 2
    count_table = lax.all_gather(own_counts.reshape(1, image_count), "dp", axis=0, tiled=True)
    ends_table = jnp.cumsum(count_table, axis=1)
    degrees = ends_table[:, -1] // slot_cap
    stub_ends = jnp.cumsum(degrees)
    stub_starts = stub_ends - degrees
    rank_ids = jnp.arange(dp_count, dtype=jnp.int32)
    is_mine = rank_ids == my_rank
    my_start = jnp.sum(jnp.where(is_mine, stub_starts, 0))
    my_degree = jnp.sum(jnp.where(is_mine, degrees, 0))
    my_ends = jnp.cumsum(own_counts)
    slot_ids = jnp.arange(slot_cap, dtype=jnp.int32)
    relative = (rank_ids - my_start) % dp_count
    live_peer = relative < my_degree
    packed_ids = relative[:, None] * slot_cap + slot_ids[None, :]
    image_of = jnp.sum((packed_ids[:, :, None] >= my_ends[None, None, :]).astype(jnp.int32), axis=2)
    image_begin = jnp.sum(
        jnp.where(
            image_of[:, :, None] == image_ids[None, None, :],
            (my_ends - own_counts)[None, None, :],
            0,
        ),
        axis=2,
    )
    target_rows = jnp.where(
        live_peer[:, None], image_of * patch_max + packed_ids - image_begin, rows_pad
    )
    outgoing = jnp.take(flat_rows, target_rows, axis=0, mode="fill", fill_value=0)
    incoming = lax.all_to_all(outgoing, "dp", split_axis=0, concat_axis=0, tiled=True)
    stub_ids = my_rank + dp_count * jnp.arange(half_count, dtype=jnp.int32)
    source_rank = jnp.sum((stub_ends[None, :] <= stub_ids[:, None]).astype(jnp.int32), axis=1)
    picked = source_rank[:, None] == rank_ids[None, :]
    source_start = jnp.sum(jnp.where(picked, stub_starts[None, :], 0), axis=1)
    source_ends = jnp.sum(jnp.where(picked[:, :, None], ends_table[None, :, :], 0), axis=1)
    source_packed = (stub_ids - source_start)[:, None] * slot_cap + slot_ids[None, :]
    source_image = jnp.sum(
        (source_packed[:, :, None] >= source_ends[:, None, :]).astype(jnp.int32), axis=2
    )
    member = (source_image[:, :, None] == image_ids[None, None, :]).astype(jnp.float32)
    work_rows = jnp.take(incoming, source_rank, axis=0).reshape(half_count * slot_cap, feat_width)
    out_rows, saved_parts = forward_rows(work_rows, params, whole_weights)
    partial_value = jnp.einsum(
        "mqi,mqd->mid",
        member,
        out_rows.reshape(half_count, slot_cap, feat_width),
        precision=lax.Precision.HIGHEST,
    )
    going_home = (
        jnp.zeros((dp_count, image_count, feat_width), jnp.float32)
        .at[source_rank]
        .set(partial_value)
    )
    pooled_sum = jnp.sum(
        lax.all_to_all(going_home, "dp", split_axis=0, concat_axis=0, tiled=True), axis=0
    )
    pooled = pooled_sum / count_f[:, None]
    img_norm = jnp.sqrt(jnp.sum(pooled * pooled, axis=1, keepdims=True) + NORM_EPS)
    img_unit = pooled / img_norm
    img_b = img_unit.astype(jnp.bfloat16)
    text_f = text_embed.astype(jnp.float32)
    txt_norm = jnp.sqrt(jnp.sum(text_f * text_f, axis=1, keepdims=True) + NORM_EPS)
    txt_unit = text_f / txt_norm
    txt_b = txt_unit.astype(jnp.bfloat16)
    logit_scale = jnp.exp(logit_params[0])
    logit_bias = logit_params[1]
    label_grid = pair_label.reshape(dp_count, blk_count, image_count)
    my_labels = label_grid[my_rank, my_blk]
    pairs_total = dp_count * blk_count * image_count

    def pair_tile(text_block, block_labels):
        inner_prod = contract_last(img_b, text_block)
        logit_vals = logit_scale * inner_prod + logit_bias
        sign_vals = jnp.where(my_labels[:, None] == block_labels[None, :], 1.0, -1.0).astype(
            jnp.float32
        )
        margins = sign_vals * logit_vals
        logit_grad = -sign_vals * jax.nn.sigmoid(-margins)
        term_sums = jnp.stack(
            [
                jnp.sum(jax.nn.softplus(-margins)),
                jnp.sum(logit_grad * logit_scale * inner_prod),
                jnp.sum(logit_grad),
            ]
        )
        image_part = logit_scale * jnp.dot(
            logit_grad, text_block.astype(jnp.float32), precision=lax.Precision.HIGHEST
        )
        text_part = logit_scale * lax.dot_general(
            logit_grad,
            img_b.astype(jnp.float32),
            (((0,), (0,)), ((), ())),
            precision=lax.Precision.HIGHEST,
        )
        return (term_sums, image_part, text_part)

    column_texts = lax.all_gather(txt_b, "dp", axis=0, tiled=True)

    def cycle_turn(turn_index, carry):
        text_block, travel, image_acc, loss_sums = carry
        source_blk = (my_blk - turn_index) % blk_count
        block_labels = lax.dynamic_index_in_dim(
            label_grid, source_blk, axis=1, keepdims=False
        ).reshape(-1)
        term_sums, image_part, text_part = pair_tile(text_block, block_labels)
        travel = travel + text_part
        text_block = from_behind(text_block, "blk", 1)
        travel = from_behind(travel, "blk", 1)
        return (text_block, travel, image_acc + image_part, loss_sums + term_sums)

    start_carry = (
        column_texts,
        jnp.zeros(column_texts.shape, jnp.float32),
        jnp.zeros((image_count, feat_width), jnp.float32),
        jnp.zeros((3,), jnp.float32),
    )
    final_carry = lax.fori_loop(0, blk_count, cycle_turn, start_carry)
    d_img = final_carry[2]
    loss_sums = final_carry[3]
    d_txt = lax.psum_scatter(final_carry[1], "dp", scatter_dimension=0, tiled=True)
    statistics = lax.psum(loss_sums, ("dp", "blk")) / pairs_total
    text_grad = (
        (d_txt - txt_unit * jnp.sum(txt_unit * d_txt, axis=1, keepdims=True)) / txt_norm
    ).astype(jnp.bfloat16)
    d_pooled = (d_img - img_unit * jnp.sum(img_unit * d_img, axis=1, keepdims=True)) / img_norm
    per_image = d_pooled / count_f[:, None]
    sent_grads = lax.all_gather(per_image, "dp", axis=0, tiled=True).reshape(
        dp_count, image_count, feat_width
    )
    source_grads = jnp.take(sent_grads, source_rank, axis=0)
    row_grad = jnp.einsum(
        "mqi,mid->mqd", member, source_grads, precision=lax.Precision.HIGHEST
    ).reshape(half_count * slot_cap, feat_width)
    row_total = backward_rows(row_grad, saved_parts, params, whole_weights)
    scaled = (patch_max * row_total).astype(jnp.bfloat16).reshape(half_count, slot_cap, feat_width)
    going_back = (
        jnp.zeros((dp_count, slot_cap, feat_width), jnp.bfloat16).at[source_rank].set(scaled)
    )
    returned = lax.all_to_all(going_back, "dp", split_axis=0, concat_axis=0, tiled=True)
    grad_flat = (
        jnp.zeros((rows_pad, feat_width), jnp.bfloat16)
        .at[target_rows.reshape(-1)]
        .set(returned.reshape(-1, feat_width), mode="drop")
    )
    patch_grad = grad_flat.reshape(1, 1, rows_pad, feat_width)
    return (patch_grad, text_grad, statistics)


def solution(mesh):
    return jax.shard_map(
        shards,
        mesh=mesh,
        in_specs=(
            P("dp", "blk", None, None),
            P("dp", "blk", None),
            P(),
            P(),
            P("dp", None),
            P(),
            P(None, "dp"),
            P(),
            P(("dp", "blk"), None),
            P(),
            P(),
        ),
        out_specs=(P("dp", "blk", None, None), P(("dp", "blk"), None), P()),
        check_vma=False,
    )
```

profile of v0, /device:TPU:1, one launch (start us, length us, event | category | flops | bytes accessed | tf_op | source)
XLA Modules:
  0.0 808.8 jit_solution(7605228553221800689)
XLA Ops:
  9.3 1.3 fusion.77
  11.3 18.6 %all-reduce = s32[32]{0:T(128)S(1)} all-reduce(s32[32]{0:T(128)S(1)} %bitcast_dynamic-update-slice_fusion), channel_id=2, replica_groups=mesh['dp'=32,'blk'=8] {'dp'}, use_global_device_ids=true, to_apply=%add | all-reduce | flops 32 | bytes 256 | tf_op jit(solution)/shard_map/squeeze | solution.py:106
  36.1 7.5 all-to-all-start
  49.1 18.3 %all-to-all-done = bf16[32,8,1152]{2,1,0:T(8,128)(2,1)S(1)} async-done(((bf16[32,8,1152]{2,1,0:T(8,128)(2,1)}), bf16[32,8,1152]{2,1,0:T(8,128)(2,1)S(1)}, u32[]{:S(2)}, u32[]{:S(2)}) %all-to-all-start) | async-done | bytes 589856 | tf_op jit(solution)/shard_map/all_to_all | solution.py:131
  68.7 65.9 %all-gather.8.cloned.1.call-done = bf16[32,36,4304]{2,1,0:T(8,128)(2,1)} async-done(((bf16[1,36,4304]{2,1,0:T(8,128)(2,1)}), bf16[32,36,4304]{2,1,0:T(8,128)(2,1)}) %all-gather.8.cloned.1.call-update) | async-done | bytes 9916432 | tf_op jit(solution)/shard_map/all_gather | solution.py:99
  134.6 14.5 %reshape.756 = bf16[1152,4304]{1,0:T(8,128)(2,1)} reshape(bf16[32,36,4304]{2,1,0:T(8,128)(2,1)} %all-gather.8.cloned.1.call-done) | data formatting | bytes 19832832
  149.2 7.2 convolution_add_fusion
  156.4 89.5 %all-gather.10.cloned.1.call-done = bf16[32,36,4304]{2,1,0:T(8,128)(2,1)} async-done(((bf16[1,36,4304]{2,1,0:T(8,128)(2,1)}), bf16[32,36,4304]{2,1,0:T(8,128)(2,1)}) %all-gather.10.cloned.1.call-update) | async-done | bytes 9916432 | tf_op jit(solution)/shard_map/all_gather | solution.py:100
  245.8 14.4 %reshape.758 = bf16[1152,4304]{1,0:T(8,128)(2,1)} reshape(bf16[32,36,4304]{2,1,0:T(8,128)(2,1)} %all-gather.10.cloned.1.call-done) | data formatting | bytes 19832832
  260.2 7.3 fusion.8
  269.5 4.6 all-to-all-start.1
  274.7 42.5 %all-gather.1 = bf16[32,1,1152]{2,1,0:T(2,128)(2,1)S(1)} all-gather(bf16[1,1,1152]{2,1,0:T(2,128)(2,1)S(1)} %get-tuple-element.392), channel_id=1, replica_groups=mesh['dp'=32,'blk'=8] {'dp'}, dimensions={0}, use_global_device_ids=true | all-gather | bytes 76032 | tf_op jit(solution)/shard_map/all_gather | solution.py:198
  317.2 1.3 constant_dynamic-slice_fusion
  320.6 82.1 %while.22 = (s32[]{:T(128)}, bf16[32,1152]{1,0:T(8,128)(2,1)S(1)}, f32[32,1152]{1,0:T(8,128)S(1)}, f32[1,1152]{1,0:T(1,128)S(1)}, f32[3]{0:T(128)}, /*index=5*/f...) while((s32[]{:T(128)}, bf16[32,1152]{1,0:T(8,128)(2,1)S(1)}, ...), condition=%wide.region_16.17_spmd.clone, body=%wide.region_12.16_spmd.clone.sunk | while | flops 631995 | bytes 1522161 | solution.py:218
  321.8 2.7 fusion.95
  327.2 2.5 fusion.97
  329.7 2.5 collective-permute-done.1
  332.3 2.8 fusion.95
  337.6 3.2 fusion.97
  341.8 2.8 fusion.95
  345.2 1.5 collective-permute-start.1
  347.6 3.2 fusion.97
  351.6 2.8 fusion.95
  357.2 3.2 fusion.97
  360.4 1.5 collective-permute-done.1
  362.0 2.8 fusion.95
  367.3 3.2 fusion.97
  370.4 2.0 collective-permute-done.1
  372.5 2.8 fusion.95
  376.9 3.2 fusion.97
  380.0 2.8 collective-permute-done.1
  383.0 2.8 fusion.95
  387.2 3.2 fusion.97
  390.4 2.8 collective-permute-done.1
  393.2 2.8 fusion.95
  397.4 3.2 fusion.97
  400.6 2.1 collective-permute-done.1
  404.0 1.3 divide_bitcast_fusion
  405.3 43.3 %all-gather.4 = f32[32,1,1152]{2,1,0:T(1,128)S(1)} all-gather(f32[1,1,1152]{2,1,0:T(1,128)S(1)} %divide_bitcast_fusion), channel_id=1, replica_groups=mesh['dp'=32,'blk'=8] {'dp'}, dimensions={0}, use_global_device_ids=true | all-gather | bytes 152064 | tf_op jit(solution)/shard_map/all_gather | solution.py:228
  450.1 17.4 %fusion.76 = (f32[128]{0:T(128)S(1)}, f32[128]{0:T(128)S(1)}, f32[128,1152]{1,0:T(8,128)}) fusion(f32[128]{0:T(128)} %copy-done.20, f32[128]{0:T(128)} %copy-done.18, bf16[16,8,1152]{2,1,0:T(8,128)(2,1)S(1)} %gather_fusion.1, pred[128]{0:T(512)(128)(4,1)} %broadcast_in_dim.164, f32[1152]{0:T(1024)} %param.15, bf16[1152,4304]{1,0:T(8,128)(2,1)} %reshape.756, ...), kind=kOutput, calls=%fused_computation.160 | convolution fusion | flops 2550544384 | bytes 23002240 | tf_op jit(solution)/shard_map/dot_general | solution.py:39
  467.6 1.4 fusion.50
  469.8 2.5 scatter_fusion
  472.3 4.1 all-to-all-start.2
  477.0 76.3 %psum.7 = f32[3]{0:T(128)S(1)} all-reduce(f32[3]{0:T(128)S(1)} %copy-done.9), channel_id=1, replica_groups=mesh['dp'=32,'blk'=8] {'dp','blk'}, use_global_device_ids=true, to_apply=%region_24.25 | all-reduce | flops 3 | bytes 24 | tf_op jit(solution)/shard_map/psum | solution.py:222
  553.9 241.3 %all-reduce.4.cloned.1.call-done = f32[32,1152]{1,0:T(8,128)} async-done(((f32[32,1152]{1,0:T(8,128)}), f32[32,1152]{1,0:T(8,128)}) %all-reduce.4.cloned.1.call-update) | async-done | bytes 147472
  795.2 2.0 multiply_reduce_fusion.2
  797.2 2.6 divide_convert_fusion
  799.8 2.5 scatter_custom_fusion.2
  (227 shorter events, 41.5 us)
Async XLA Ops:
  7.2 26.5 %copy-start = (bf16[1,1,256,1152]{3,2,1,0:T(8,128)(2,1)S(1)}, bf16[1,1,256,1152]{3,2,1,0:T(8,128)(2,1)}, u32[]{:S(2)}) copy-start(bf16[1,1,256,1152]{3,2,1,0:T(8,128)(2,1)} %param.13) | copy-start | bytes 1769476
  7.2 127.4 %all-gather.8.cloned.1.call-start = ((), (), s32[]{:S(2)}) async-start(), calls=%async_computation.3 | async-start | bytes 11489280 | tf_op jit(solution)/shard_map/all_gather | solution.py:99
  7.9 237.9 %all-gather.10.cloned.1.call-start = ((), (), s32[]{:S(2)}) async-start(), calls=%async_computation.4 | async-start | bytes 11489280 | tf_op jit(solution)/shard_map/all_gather | solution.py:100
  32.2 2.8 copy-start.11
  33.5 1.5 copy-start.22
  35.0 8.7 %copy-start.8 = (bf16[1,1152]{1,0:T(2,128)(2,1)S(1)}, bf16[1,1152]{1,0:T(2,128)(2,1)}, u32[]{:S(2)}) copy-start(bf16[1,1152]{1,0:T(2,128)(2,1)} %param.21) | copy-start | bytes 6916
  35.0 10.0 %copy-start.26 = (f32[2]{0:T(128)S(1)}, f32[2]{0:T(128)}, u32[]{:S(2)}) copy-start(f32[2]{0:T(128)} %param.23) | copy-start | bytes 28
  35.0 12.2 %copy-start.27 = (s32[256]{0:T(256)S(1)}, s32[256]{0:T(256)}, u32[]{:S(2)}) copy-start(s32[256]{0:T(256)} %param.22) | copy-start | bytes 3076
  36.1 31.3 %all-to-all-start = ((bf16[32,8,1152]{2,1,0:T(8,128)(2,1)}), bf16[32,8,1152]{2,1,0:T(8,128)(2,1)S(1)}, u32[]{:S(2)}, u32[]{:S(2)}) async-start(bf16[32,8,1152]{2,1,0:T(8,128)(2,1)} %bitcast_select_fusion), calls=%async_computation | async-start | bytes 1179648 | tf_op jit(solution)/shard_map/all_to_all | solution.py:131
  46.5 102.6 %copy-start.10 = (pred[16]{0:T(512)(128)(4,1)}, pred[16]{0:T(512)(128)(4,1)S(1)}, u32[]{:S(2)}) copy-start(pred[16]{0:T(512)(128)(4,1)S(1)} %compare_and_fusion.1) | copy-start | bytes 52
  47.3 1.7 copy-start.3
  48.0 86.6 %copy-start.15 = (s32[1024]{0:T(1024)}, s32[1024]{0:T(1024)S(1)}, u32[]{:S(2)}) copy-start(s32[1024]{0:T(1024)S(1)} %pad_clamp_fusion) | copy-start | bytes 12292
  68.2 80.9 %copy-start.18 = (f32[128]{0:T(128)}, f32[128]{0:T(128)S(1)}, u32[]{:S(2)}) copy-start(f32[128]{0:T(128)S(1)} %div.127) | copy-start | bytes 1540
  68.6 80.5 %copy-start.20 = (f32[128]{0:T(128)}, f32[128]{0:T(128)S(1)}, u32[]{:S(2)}) copy-start(f32[128]{0:T(128)S(1)} %rsqrt.12) | copy-start | bytes 1540
  68.6 80.5 %copy-start.7 = (f32[4304]{0:T(1024)S(1)}, f32[4304]{0:T(1024)}, u32[]{:S(2)}) copy-start(f32[4304]{0:T(1024)} %param.18) | copy-start | bytes 51652
  68.7 80.5 %copy-start.13 = (f32[1152]{0:T(1024)S(1)}, f32[1152]{0:T(1024)}, u32[]{:S(2)}) copy-start(f32[1152]{0:T(1024)} %param.16) | copy-start | bytes 13828
  68.7 80.5 %copy-start.14 = (f32[1152]{0:T(1024)S(1)}, f32[1152]{0:T(1024)}, u32[]{:S(2)}) copy-start(f32[1152]{0:T(1024)} %param.15) | copy-start | bytes 13828
  68.7 80.5 %copy-start.16 = (pred[128]{0:T(512)(128)(4,1)S(1)}, pred[128]{0:T(512)(128)(4,1)}, u32[]{:S(2)}) copy-start(pred[128]{0:T(512)(128)(4,1)} %broadcast_in_dim.164) | copy-start | bytes 388
  156.3 103.9 %copy-start.28 = (f32[1152]{0:T(1024)S(1)}, f32[1152]{0:T(1024)}, u32[]{:S(2)}) copy-start(f32[1152]{0:T(1024)} %param.20) | copy-start | bytes 13828
  269.5 49.1 %all-to-all-start.1 = ((f32[32,1,1152]{2,1,0:T(1,128)}), f32[32,1,1152]{2,1,0:T(1,128)S(1)}, u32[]{:S(2)}, u32[]{:S(2)}) async-start(f32[32,1,1152]{2,1,0:T(1,128)} %reshape.721), calls=%async_computation.1 | async-start | bytes 294912 | tf_op jit(solution)/shard_map/all_to_all | solution.py:156
  320.6 9.1 %collective-permute-start = (bf16[32,1152]{1,0:T(8,128)(2,1)S(1)}, bf16[32,1152]{1,0:T(8,128)(2,1)S(1)}, u32[]{:S(2)}, u32[]{:S(2)}) collective-permute-start(bf16[32,1152]{1,0:T(8,128)(2,1)S(1)} %copy.49), channel_id=1, source_target_pairs={{0,1},{1,2},{2,3},{3,4},{4,5},{5,6},{6,7},{7,0},{8,9},{9,10},{10,1... | collective-permute-start | bytes 221192 | tf_op jit(solution)/shard_map/while/body/eval_jaxpr/ppermute | solution.py:17
  325.1 7.1 collective-permute-start.1
  332.2 8.6 %collective-permute-start = (bf16[32,1152]{1,0:T(8,128)(2,1)S(1)}, bf16[32,1152]{1,0:T(8,128)(2,1)S(1)}, u32[]{:S(2)}, u32[]{:S(2)}) collective-permute-start(bf16[32,1152]{1,0:T(8,128)(2,1)S(1)} %copy.49), channel_id=1, source_target_pairs={{0,1},{1,2},{2,3},{3,4},{4,5},{5,6},{6,7},{7,0},{8,9},{9,10},{10,1... | collective-permute-start | bytes 221192 | tf_op jit(solution)/shard_map/while/body/eval_jaxpr/ppermute | solution.py:17
  335.6 6.1 collective-permute-start.1
  341.7 9.0 %collective-permute-start = (bf16[32,1152]{1,0:T(8,128)(2,1)S(1)}, bf16[32,1152]{1,0:T(8,128)(2,1)S(1)}, u32[]{:S(2)}, u32[]{:S(2)}) collective-permute-start(bf16[32,1152]{1,0:T(8,128)(2,1)S(1)} %copy.49), channel_id=1, source_target_pairs={{0,1},{1,2},{2,3},{3,4},{4,5},{5,6},{6,7},{7,0},{8,9},{9,10},{10,1... | collective-permute-start | bytes 221192 | tf_op jit(solution)/shard_map/while/body/eval_jaxpr/ppermute | solution.py:17
  345.2 6.3 collective-permute-start.1
  351.5 8.8 %collective-permute-start = (bf16[32,1152]{1,0:T(8,128)(2,1)S(1)}, bf16[32,1152]{1,0:T(8,128)(2,1)S(1)}, u32[]{:S(2)}, u32[]{:S(2)}) collective-permute-start(bf16[32,1152]{1,0:T(8,128)(2,1)S(1)} %copy.49), channel_id=1, source_target_pairs={{0,1},{1,2},{2,3},{3,4},{4,5},{5,6},{6,7},{7,0},{8,9},{9,10},{10,1... | collective-permute-start | bytes 221192 | tf_op jit(solution)/shard_map/while/body/eval_jaxpr/ppermute | solution.py:17
  355.0 6.9 collective-permute-start.1
  361.9 8.5 %collective-permute-start = (bf16[32,1152]{1,0:T(8,128)(2,1)S(1)}, bf16[32,1152]{1,0:T(8,128)(2,1)S(1)}, u32[]{:S(2)}, u32[]{:S(2)}) collective-permute-start(bf16[32,1152]{1,0:T(8,128)(2,1)S(1)} %copy.49), channel_id=1, source_target_pairs={{0,1},{1,2},{2,3},{3,4},{4,5},{5,6},{6,7},{7,0},{8,9},{9,10},{10,1... | collective-permute-start | bytes 221192 | tf_op jit(solution)/shard_map/while/body/eval_jaxpr/ppermute | solution.py:17
  365.4 7.1 collective-permute-start.1
  372.5 7.6 collective-permute-start
  375.9 7.0 collective-permute-start.1
  382.9 7.5 collective-permute-start
  386.3 6.8 collective-permute-start.1
  393.1 7.4 collective-permute-start
  396.5 6.1 collective-permute-start.1
  402.6 64.8 %copy-start.1 = (f32[32,1152]{1,0:T(8,128)}, f32[32,1152]{1,0:T(8,128)S(1)}, u32[]{:S(2)}) copy-start(f32[32,1152]{1,0:T(8,128)S(1)} %get-tuple-element.271) | copy-start | bytes 442372
  450.0 17.5 %copy-start.6 = (f32[16,8]{1,0:T(8,128)S(1)}, f32[16,8]{1,0:T(8,128)}, u32[]{:S(2)}) copy-start(f32[16,8]{1,0:T(8,128)} %get-tuple-element.399) | copy-start | bytes 1540
  450.0 17.5 %copy-start.17 = (pred[128]{0:T(512)(128)(4,1)S(1)}, pred[128]{0:T(512)(128)(4,1)}, u32[]{:S(2)}) copy-start(pred[128]{0:T(512)(128)(4,1)} %broadcast_in_dim.164) | copy-start | bytes 388
  450.0 17.5 %copy-start.19 = (f32[128]{0:T(128)S(1)}, f32[128]{0:T(128)}, u32[]{:S(2)}) copy-start(f32[128]{0:T(128)} %copy-done.18) | copy-start | bytes 1540
  450.1 17.5 %copy-start.21 = (f32[128]{0:T(128)S(1)}, f32[128]{0:T(128)}, u32[]{:S(2)}) copy-start(f32[128]{0:T(128)} %copy-done.20) | copy-start | bytes 1540
  450.1 19.7 %copy-start.25 = (s32[16]{0:T(128)S(1)}, s32[16]{0:T(128)}, u32[]{:S(2)}) copy-start(s32[16]{0:T(128)} %copy-done.24) | copy-start | bytes 196
  467.5 9.0 %copy-start.23 = (pred[32]{0:T(512)(128)(4,1)S(1)}, pred[32]{0:T(512)(128)(4,1)}, u32[]{:S(2)}) copy-start(pred[32]{0:T(512)(128)(4,1)} %copy-done.22) | copy-start | bytes 100
  467.5 9.2 %copy-start.12 = (s32[32]{0:T(128)S(1)}, s32[32]{0:T(128)}, u32[]{:S(2)}) copy-start(s32[32]{0:T(128)} %copy-done.11) | copy-start | bytes 388
  467.5 9.5 %copy-start.9 = (f32[3]{0:T(128)S(1)}, f32[3]{0:T(128)}, u32[]{:S(2)}) copy-start(f32[3]{0:T(128)} %get-tuple-element.272) | copy-start | bytes 40
  467.5 327.8 %copy-start.5 = (f32[1,1152]{1,0:T(1,128)S(1)}, f32[1,1152]{1,0:T(1,128)}, u32[]{:S(2)}) copy-start(f32[1,1152]{1,0:T(1,128)} %get-tuple-element.393) | copy-start | bytes 13828
  472.3 327.6 %all-to-all-start.2 = ((bf16[32,8,1152]{2,1,0:T(8,128)(2,1)}), bf16[32,8,1152]{2,1,0:T(8,128)(2,1)S(1)}, u32[]{:S(2)}, u32[]{:S(2)}) async-start(bf16[32,8,1152]{2,1,0:T(8,128)(2,1)} %scatter_fusion), calls=%async_computation.2 | async-start | bytes 1179648 | tf_op jit(solution)/shard_map/all_to_all | solution.py:240
  476.4 318.8 %all-reduce.4.cloned.1.call-start = ((), (), s32[]{:S(2)}) async-start(), calls=%async_computation.5 | async-start | bytes 294912
  (10 other events, 6.3 us)
Sparse Core Ops, SparseCore 0:
  10.7 123.8 all-gather.7
  137.3 108.4 all-gather.9
  553.5 241.6 all-reduce.3
where the time goes:
time: 811 us; the launch traced here: 809 us
  waiting for transfers between devices  432 us (53%)
  blocking collectives  181 us (22%)
  matrix products  61.1 us (8%)
  local copies, waits for them, and re-layouts  49.8 us (6%)
  other arithmetic  43.9 us (5%)
  starting transfers between devices  23.9 us (3%)
  between operations  17 us (2%)
    unnamed x4, waiting for transfers between devices  243 us
    all_gather x1, waiting for transfers between devices, shards(): lax.all_gather(weight_out, 'dp', axis=1, tiled=True)  89.5 us
    psum x1, blocking collectives, shards(): statistics = lax.psum(loss_sums, ('dp', 'blk')) / pairs_total  76.3 us
    all_gather x1, waiting for transfers between devices, shards(): lax.all_gather(weight_in, 'dp', axis=0, tiled=True)  65.9 us
    all_gather x1, blocking collectives, shards(): lax.all_gather(per_image, 'dp', axis=0, tiled=True)  43.3 us
    all_gather x1, blocking collectives, shards(): column_texts = lax.all_gather(txt_b, 'dp', axis=0, tiled=True)  42.5 us
    dot_general x9, matrix products, contract_last(): lax.dot_general(left, right, (((1,), (1,)), ((), ())), preferred_element_...  39.6 us
    unnamed x64, local copies, waits for them, and re-layouts  32.3 us
  transfers between devices with their start and end apart: 22, of which 12 were waited for; matrix products, arithmetic and copies ran while one was open for 12% of the time, Pallas kernels for 0%

commit v1 on v0

v1 whole, which is shorter than its diff:
```python
import jax
import jax.numpy as jnp
from jax import lax
from jax.experimental import pallas as pl
from jax.experimental.pallas import tpu as pltpu
from jax.sharding import PartitionSpec as P

D = 1152
FF = 4304
ROWS = 256
NORM_EPS = 1e-06
GELU_SCALE = 0.7978845608028654
GELU_CUBIC = 0.044715
MESH = pl.DeviceIdType.MESH
F32 = jnp.float32
BF16 = jnp.bfloat16
NT_IN = 34
N_COPIES = 180


def dev(x, y, z, c):
    x, y, z, c = x % 4, y % 4, z % 8, c % 2
    return ((y // 2) * 16 + z * 2 + c, x * 2 + y % 2)


def nt_dot(a, b):
    return lax.dot_general(a, b, (((1,), (1,)), ((), ())), preferred_element_type=F32)


def nn_dot(a, b):
    return jnp.dot(a, b, preferred_element_type=F32)


def split3(v):
    hi = v.astype(BF16)
    rest = v - hi.astype(F32)
    mid = rest.astype(BF16)
    low = (rest - mid.astype(F32)).astype(BF16)
    return hi, mid, low


def exact_dot(v, w, dot):
    rows = v.shape[0]
    hi, mid, low = split3(v)
    res = dot(jnp.concatenate([hi, mid, low], axis=0), w)
    return res[:rows] + res[rows : 2 * rows] + res[2 * rows :]


def rows8(v):
    return jnp.broadcast_to(v, (8, v.shape[1]))


def kernel(
    x_ref, wi_ref, wo_ref, vec_ref, bin_ref, labl_ref, lab2_ref, sc_ref,
    out_ref, tg_ref, st_ref,
    G, W, PM, XP, PLAIN, RSTD, NM, SL, HS, AF, ACC, RW, RO, SF, VP,
    TROW, TCOL, TB, HA, PB, PR, GB, AB, AR, ICOL, DB, DT,
    SS, RS,
):
    dp, blk = lax.axis_index("dp"), lax.axis_index("blk")
    yh, z, c = dp // 16, (dp // 2) % 8, dp % 2
    x, yl = blk // 2, blk % 2
    y = yh * 2 + yl
    cross = dev(x, y + 3 + 2 * yl, z, c)
    share = dev(x, yh * 2 + 1 - yl, z, c)
    partner = dev(x, y, z, c + 1)
    zp, zm = dev(x, y, z + 1, c), dev(x, y, z + 7, c)
    xp, xm = dev(x + 1, y, z, c), dev(x + 3, y, z, c)
    u, v, s = z * 2 + c, x * 4 + y, x * 2 + c
    col_peers = [((u + d) % 16) for d in range(1, 16)]
    col_devs = [dev(x, y, p // 2, p % 2) for p in col_peers]
    plane_peers = [((v + d) % 16) for d in range(1, 16)]
    plane_devs = [dev(p // 4, p % 4, z, c) for p in plane_peers]
    ring_peers = [((s + d) % 8) for d in range(1, 8)]
    ring_devs = [dev(p // 2, y, z, p % 2) for p in ring_peers]

    bar = pltpu.get_barrier_semaphore()
    greet = col_devs + plane_devs + [dev(x + d, y, z, c + 1) for d in (1, 2, 3)]
    for peer in greet:
        pl.semaphore_signal(bar, inc=1, device_id=peer, device_id_type=MESH)

    copies = {}

    def send(name, src, dst, device):
        k = len(copies)
        cp = pltpu.make_async_remote_copy(
            src_ref=src, dst_ref=dst, send_sem=SS.at[k], recv_sem=RS.at[k], device_id=device, device_id_type=MESH
        )
        cp.start()
        copies[name] = cp

    def same(name, ref, device):
        send(name, ref, ref, device)

    def got(name):
        copies[name].wait_recv()

    def fold(rows, first, count):
        parts = []
        for a in range(0, 8, 2):
            blocks = []
            for b in range(2):
                if a + b < count:
                    t = first + a + b
                    piece = rows[:, 128 * t : 128 * t + 128]
                    blocks.append(pltpu.roll(piece, 4, 0) if b else piece)
            parts.append(sum(blocks) if blocks else jnp.zeros((8, 128), F32))
        return jnp.concatenate(parts, axis=0).astype(BF16)

    wi_tail = wi_ref[32:48, :].astype(F32)[0:8]
    for q in range(4):
        for t in range(8):
            G[yh, z, c, q, 5 * (t // 4) + t % 4] = wi_ref[0:32, 1024 * q + 128 * t : 1024 * q + 128 * t + 128]
        G[yh, z, c, q, 4] = fold(wi_tail, 8 * q, 8)
    eye = (
        lax.broadcasted_iota(jnp.int32, (48, 36), 0) == lax.broadcasted_iota(jnp.int32, (48, 36), 1)
    ).astype(F32).astype(BF16)
    wo_first = 8 * x + x // 2
    wo_rows = wo_ref[pl.ds(pl.multiple_of(128 * wo_first, 128), 1152), :]
    wo_t = nt_dot(eye, wo_rows)
    wo_main = wo_t[0:32].astype(BF16)
    for t in range(2):
        W[yh, z, c, t] = wi_ref[0:32, 4096 + 128 * t : 4096 + 128 * t + 128]
    for t in range(9):
        W[yh, z, c, 2 + t] = wo_main[:, 128 * t : 128 * t + 128]
    tail = jnp.concatenate([wi_tail[:, 4096:4352], wo_t[32:40]], axis=1)
    W[yh, z, c, 11] = fold(tail, 0, 8)
    W[yh, z, c, 12] = fold(tail, 8, 3)

    pl.semaphore_wait(bar, len(greet))

    def zz(d):
        return (z + 8 + d) % 8

    other = 1 - yh
    both = slice(None)
    mine5 = pl.ds(4 * yl, 5)
    mine4 = pl.ds(5 * yl, 4)
    pair0 = 2 * (x // 2)
    pair1 = 2 - pair0

    def z_in(n):
        if n < 4:
            got(("zR", n - 1))
            got(("zL", n - 1))
            if n == 1:
                got(("zRb", 0))
                got(("zLb", 0))
            sel_r = both if n < 3 else 0
            sel_l = both if n < 3 else 1
            same(("zR", n), G.at[sel_r, zz(-n), c, x, mine5], zp)
            same(("zL", n), G.at[sel_l, zz(n), c, x, mine5], zm)
        else:
            got(("zR", 3))
            got(("zL", 3))

    def d_in(n):
        if n == 0:
            got(("d1",))
        else:
            got(("dR", n - 1))
            got(("dL", n - 1))
        if n < 4:
            sel_r = both if n < 3 else 0
            sel_l = both if n < 3 else 1
            same(("dR", n), W.at[sel_r, zz(-n), c], zp)
            same(("dL", n), W.at[sel_l, zz(n), c], zm)

    def d_partner(dz):
        same(("pD", dz), W.at[:, zz(dz), c], partner)

    def x_send(dz):
        sel = other if dz == 0 else both
        same(("xR", dz), G.at[sel, zz(dz), c, x, mine5], xp)
        same(("xL", dz), G.at[sel, zz(dz), c, x, mine5], xm)

    def x_in(dz):
        got(("xR", dz))
        got(("xL", dz))
        same(("fR", dz), G.at[other if dz == 0 else 0, zz(dz), c, (x + 3) % 4, mine5], xp)
        if dz != 0:
            same(("fL", dz), G.at[1, zz(dz), c, (x + 1) % 4, mine5], xm)
            same(("yC", dz), G.at[:, zz(dz), c, pl.ds(pair0, 2), mine4], cross)

    def f_in(dz):
        got(("fR", dz))
        if dz != 0:
            got(("fL", dz))
        sel = other if dz == 0 else both
        same(("yS", dz), G.at[sel, zz(dz), c, pl.ds(pair1, 2), mine4], share)

    def y_in(dz):
        got(("yC", dz))
        got(("yS", dz))
        same(("pG", dz), G.at[:, zz(dz), c], partner)

    same(("e1",), G.at[yh, z, c, x, pl.ds(4 * (1 - yl), 5)], cross)
    same(("zR", 0), G.at[yh, z, c, x, mine5], zp)
    same(("zL", 0), G.at[yh, z, c, x, mine5], zm)
    same(("yC", 0), G.at[yh, z, c, pl.ds(pair0, 2), mine4], cross)
    same(("d1",), W.at[yh, z, c], cross)

    lane = lax.broadcasted_iota(jnp.int32, (1, D), 1)
    rest = lane - 1024
    natural = jnp.where(lane < 1024, 36 * (lane >> 5) + (lane & 31), 36 * (rest >> 2) + 32 + (rest & 3))

    @pl.loop(0, 9)
    def _(i):
        first = pl.multiple_of(128 * i, 128)
        rows = lax.broadcasted_iota(jnp.int32, (128, D), 0) + 128 * i
        PM[pl.ds(first, 128), :] = jnp.where(rows == natural, 1.0, 0.0).astype(BF16)

    got(("e1",))
    same(("zRb", 0), G.at[other, z, c, x, mine5], zp)
    same(("zLb", 0), G.at[other, z, c, x, mine5], zm)
    x_send(0)

    VP[...] = exact_dot(vec_ref[...], PM[...], nn_dot)
    gain, nbias, bout, text_f = VP[0:1, :], VP[1:2, :], VP[2:3, :], VP[3:4, :]
    txt_norm = jnp.sqrt(jnp.sum(text_f * text_f, axis=1, keepdims=True) + NORM_EPS)
    txt_unit = text_f / txt_norm
    TROW[...] = txt_unit
    TCOL[u] = jnp.concatenate([txt_unit.astype(BF16).astype(F32), jnp.zeros((1, 128), F32)], axis=1)
    for i, device in enumerate(col_devs):
        same(("t1", i), TCOL.at[u], device)

    z_in(1)
    x_send(-1)
    x_send(1)
    x_in(0)

    count = sc_ref[2:3, 0:1]

    @pl.loop(0, 4)
    def _(i):
        rows = pl.ds(pl.multiple_of(64 * i, 64), 64)
        xs = nn_dot(x_ref[rows, :], PM[...])
        XP[rows, :] = xs
        centre = xs - jnp.mean(xs, axis=1, keepdims=True)
        inv = lax.rsqrt(jnp.mean(centre * centre, axis=1, keepdims=True) + NORM_EPS)
        plain = centre * inv
        PLAIN[rows, :] = plain
        RSTD[rows, :] = jnp.broadcast_to(inv, (64, 128))
        NM[rows, :] = (plain * gain + nbias).astype(BF16)

    f_in(0)
    for i in range(15):
        got(("t1", i))
    block = TCOL[...].reshape(16, 1280).astype(BF16)
    TB[c, v] = jnp.where(c == 0, block[:, :640].astype(F32), block[:, 640:].astype(F32)).astype(BF16)
    for i, device in enumerate(plane_devs):
        same(("t2", i), TB.at[c, v], device)

    z_in(2)
    x_send(-2)
    x_send(2)
    x_in(-1)
    x_in(1)
    y_in(0)
    z_in(3)
    x_send(-3)
    x_send(3)
    x_in(-2)
    x_in(2)
    f_in(-1)
    f_in(1)
    z_in(4)
    x_send(4)
    d_in(0)
    y_in(-1)
    y_in(1)
    d_partner(0)
    x_in(-3)
    x_in(3)
    f_in(-2)
    f_in(2)
    y_in(-2)
    y_in(2)
    for i in range(15):
        got(("t2", i))
    same(("t3",), TB.at[c], partner)

    row_ids = lax.broadcasted_iota(jnp.int32, (ROWS, 1), 0).astype(F32)
    valid = row_ids < count
    xsum = jnp.sum(jnp.where(valid, XP[...], 0.0), axis=0, keepdims=True)

    @pl.loop(0, 8)
    def _(i):
        r = lax.broadcasted_iota(jnp.int32, (128, 1024), 0)
        col = lax.broadcasted_iota(jnp.int32, (128, 1024), 1)
        SF[pl.ds(pl.multiple_of(128 * i, 128), 128), :] = jnp.where(
            col == 32 * (r >> 2) + 4 * i + (r & 3), 1.0, 0.0
        ).astype(BF16)

    x_in(4)
    f_in(-3)
    f_in(3)
    d_in(1)
    d_partner(-1)
    d_partner(1)
    y_in(-3)
    y_in(3)
    f_in(4)
    d_in(2)
    d_partner(-2)
    d_partner(2)
    y_in(4)
    d_in(3)
    d_partner(-3)
    d_partner(3)
    d_in(4)
    d_partner(4)
    order = (0, -1, 1, -2, 2, -3, 3, 4)
    for dz in order:
        got(("pG", dz))
    for dz in order:
        got(("pD", dz))
    got(("t3",))

    def unfold(store, pieces):
        res = nn_dot(SF[...], jnp.concatenate([p.reshape(1024, 128) for p in pieces], axis=1)).astype(BF16)
        for j in range(len(pieces)):
            for a in range(8):
                store(j, a, res[128 * a : 128 * a + 128, 128 * j : 128 * j + 128])

    def store_in(base):
        def store(j, a, tile):
            RW[8 * (base + j) + a] = tile
        return store

    def store_direct(j, a, tile):
        t = 8 * j + a
        if t < 2:
            RW[32 + t] = tile
        elif t < 11:
            RO[t - 2] = tile

    for q in (0, 2):
        unfold(store_in(q), [G[:, :, :, q, 4], G[:, :, :, q + 1, 4]])
    unfold(store_direct, [W[:, :, :, 11], W[:, :, :, 12]])

    def fwd(first, count_tiles, main_tiles):
        wm = jnp.concatenate([m.reshape(1024, 128) for m in main_tiles], axis=1)
        wr = jnp.concatenate([RW[first + t] for t in range(count_tiles)], axis=1)
        pre_all = nn_dot(NM[:, :1024], wm) + nn_dot(NM[:, 1024:], wr)
        for t in range(count_tiles):
            pre = pre_all[:, 128 * t : 128 * t + 128] + bin_ref[first + t]
            sq = pre * pre
            th = jnp.tanh(GELU_SCALE * pre * (1.0 + GELU_CUBIC * sq))
            half = 0.5 * (1.0 + th)
            hid = pre * half
            SL[first + t] = half + 0.5 * pre * (1.0 - th * th) * (GELU_SCALE + 3.0 * GELU_SCALE * GELU_CUBIC * sq)
            HS[first + t] = jnp.sum(jnp.where(valid, hid, 0.0), axis=0, keepdims=True)

    @pl.loop(0, 8)
    def _(p):
        q, half = p // 2, p % 2
        fwd(4 * p, 4, [G[:, :, :, q, 5 * half + t] for t in range(4)])

    fwd(32, 2, [W[:, :, :, 0], W[:, :, :, 1]])

    def first_tile(member):
        return 4 * member + member // 4

    for i, (p, device) in enumerate(zip(ring_peers, ring_devs)):
        send(("h", i), HS.at[pl.ds(first_tile(p), 5)], HA.at[s], device)
    HA[s] = HS[pl.ds(first_tile(s), 5)]
    for i in range(7):
        got(("h", i))
    last_mine = jnp.where(s % 4 == 3, 1.0, 0.0)
    part_m = jnp.zeros((24, 1024), F32)
    part_r = jnp.zeros((24, 128), F32)
    for t in range(5):
        col = HA[:, t].reshape(8, 128)
        if t == 4:
            col = col * last_mine
        lhs = jnp.concatenate(split3(col), axis=0)
        part_m += nt_dot(lhs, W[:, :, :, 2 + 4 * c + t].reshape(1024, 128))
        part_r += nt_dot(lhs, RO[4 * c + t])
    part = jnp.concatenate([part_m, part_r], axis=1)
    part = part[0:8] + part[8:16] + part[16:24]
    for j in range(8):
        PB[j] = part[j : j + 1]
    for i, (p, device) in enumerate(zip(ring_peers, ring_devs)):
        send(("p", i), PB.at[p], PR.at[s], device)
    PR[s] = PB[s]
    for i in range(7):
        got(("p", i))
    mixed = jnp.sum(PR[...].reshape(8, D), axis=0, keepdims=True)
    pooled = (xsum + mixed) / count + bout

    img_norm = jnp.sqrt(jnp.sum(pooled * pooled, axis=1, keepdims=True) + NORM_EPS)
    img_unit = pooled / img_norm
    img_b = img_unit.astype(BF16)
    scale = jnp.exp(sc_ref[0:1, 0:1])
    shift = sc_ref[1:2, 0:1]
    texts = jnp.concatenate([TB[0].reshape(256, 640), TB[1].reshape(256, 640)[:, :512]], axis=1)

    def terms(inner, same_label):
        logits = scale * inner + shift
        sign = jnp.where(same_label, 1.0, -1.0)
        neg = -sign * logits
        soft = jnp.maximum(neg, 0.0) + jnp.log1p(jnp.exp(-jnp.abs(neg)))
        return soft, -sign / (1.0 + jnp.exp(-neg))

    inner = nt_dot(jnp.broadcast_to(img_b.astype(F32), (16, D)).astype(BF16), texts)[0:8]
    labels = labl_ref[...]
    lane256 = lax.broadcasted_iota(jnp.int32, (1, 256), 1)
    own_label = jnp.sum(jnp.where(lane256 == v * 16 + u, labels, 0.0), axis=1, keepdims=True)
    soft, grad = terms(inner, labels == own_label)
    stats = [
        jnp.sum(soft[0:1], axis=1, keepdims=True),
        jnp.sum((grad * scale * inner)[0:1], axis=1, keepdims=True),
        jnp.sum(grad[0:1], axis=1, keepdims=True),
    ]
    lane128 = lax.broadcasted_iota(jnp.int32, (1, 128), 1)
    stat_row = sum(jnp.where(lane128 == k, stats[k], 0.0) for k in range(3))
    ICOL[u] = jnp.concatenate([img_b.astype(F32), stat_row], axis=1)
    for i, device in enumerate(col_devs):
        same(("i1", i), ICOL.at[u], device)

    d_img = scale * exact_dot(grad, texts, nn_dot)[0:1]
    d_pooled = (d_img - img_unit * jnp.sum(img_unit * d_img, axis=1, keepdims=True)) / img_norm
    row_grad = d_pooled / count

    GB[s] = row_grad
    for i, device in enumerate(ring_devs):
        same(("g", i), GB.at[s], device)
    for i in range(7):
        got(("g", i))
    grads = GB[...].reshape(8, D).astype(BF16)
    for t in range(5):
        res = nn_dot(grads[:, :1024], W[:, :, :, 2 + 4 * c + t].reshape(1024, 128)) + nn_dot(
            grads[:, 1024:], RO[4 * c + t]
        )
        for j in range(8):
            AB[j, t] = res[j : j + 1]
    for i, (p, device) in enumerate(zip(ring_peers, ring_devs)):
        send(("a", i), AB.at[p], AR.at[s], device)
    AR[s] = AB[s]

    for i in range(15):
        got(("i1", i))
    column = ICOL[...].reshape(16, 1280)
    imgs = column[:, :D].astype(BF16)
    pick = (
        lax.broadcasted_iota(jnp.int32, (16, 256), 1) == 16 * lax.broadcasted_iota(jnp.int32, (16, 256), 0) + u
    )
    texts16 = nn_dot(jnp.where(pick, 1.0, 0.0).astype(BF16), texts).astype(BF16)
    lab2 = lab2_ref[...]
    lab_txt = jnp.sum(
        jnp.where(lax.broadcasted_iota(jnp.int32, (16, 128), 1) == u, lab2, 0.0), axis=1, keepdims=True
    )
    lab_img = jnp.sum(
        jnp.where(lax.broadcasted_iota(jnp.int32, (16, 128), 0) == v, lab2, 0.0), axis=0, keepdims=True
    )[:, :16]
    _, grad_t = terms(nt_dot(texts16, imgs), lab_txt == lab_img)
    d_part = exact_dot(grad_t, imgs, nn_dot)
    col_stats = jnp.sum(column[:, D:], axis=0, keepdims=True)
    for k in range(16):
        DB[k] = jnp.concatenate([d_part[k : k + 1], col_stats], axis=1)
    for i, (p, device) in enumerate(zip(plane_peers, plane_devs)):
        send(("i2", i), DB.at[p], DT.at[v], device)
    DT[v] = DB[v]

    for i in range(7):
        got(("a", i))

    def act_tile(t):
        member = 0
        while member < 7 and first_tile(member + 1) <= t:
            member += 1
        return AR[member, t - first_tile(member)]

    for t in range(NT_IN):
        AF[t] = act_tile(t)

    def bwd(first, count_tiles, main_tiles, start):
        pg = jnp.concatenate([(AF[first + t] * SL[first + t]).astype(BF16) for t in range(count_tiles)], axis=1)
        wm = jnp.concatenate([m.reshape(1024, 128) for m in main_tiles], axis=1)
        wr = jnp.concatenate([RW[first + t] for t in range(count_tiles)], axis=1)
        if start:
            ACC[:, :1024] = nt_dot(pg, wm)
            ACC[:, 1024:] = nt_dot(pg, wr)
        else:
            ACC[:, :1024] += nt_dot(pg, wm)
            ACC[:, 1024:] += nt_dot(pg, wr)

    bwd(32, 2, [W[:, :, :, 0], W[:, :, :, 1]], True)

    @pl.loop(0, 8)
    def _(p):
        q, half = p // 2, p % 2
        bwd(4 * p, 4, [G[:, :, :, q, 5 * half + t] for t in range(4)], False)

    @pl.loop(0, 4)
    def _(i):
        rows = pl.ds(pl.multiple_of(64 * i, 64), 64)
        plain = PLAIN[rows, :]
        q = ACC[rows, :] * VP[0:1, :]
        mean_q = jnp.mean(q, axis=1, keepdims=True)
        mean_qp = jnp.mean(q * plain, axis=1, keepdims=True)
        total = row_grad + RSTD[rows, 0:1] * (q - mean_q - plain * mean_qp)
        ids = (lax.broadcasted_iota(jnp.int32, (64, 1), 0) + 64 * i).astype(F32)
        scaled = jnp.where(ids < count, 256.0 * total, 0.0).astype(BF16)
        out_ref[rows, :] = nt_dot(scaled, PM[...]).astype(BF16)

    for i in range(15):
        got(("i2", i))
    sums = jnp.sum(DT[...].reshape(16, 1280), axis=0, keepdims=True)
    st_ref[...] = sums[:, D:] / 256.0
    d_txt = scale * sums[:, :D]
    unit = TROW[...]
    tg = (d_txt - unit * jnp.sum(unit * d_txt, axis=1, keepdims=True)) / jnp.sqrt(
        jnp.sum(VP[3:4, :] * VP[3:4, :], axis=1, keepdims=True) + NORM_EPS
    )
    tg_ref[...] = nt_dot(jnp.broadcast_to(tg, (16, D)).astype(BF16), PM[...])[0:1].astype(BF16)

    for cp in copies.values():
        cp.wait_send()


def shards(
    patches, counts, norm_gain, norm_bias, weight_in, bias_in, weight_out, bias_out, text_embed, pair_label,
    logit_params,
):
    rows = patches.reshape(ROWS, D)
    wi = jnp.pad(weight_in, ((0, 12), (0, 48)))
    wo = jnp.pad(weight_out, ((0, 48), (0, 0)))
    vec = jnp.concatenate(
        [norm_gain[None], norm_bias[None], bias_out[None], text_embed.astype(F32), jnp.zeros((4, D), F32)], axis=0
    )
    bias = jnp.pad(bias_in, (0, 48)).reshape(NT_IN, 1, 128)
    labels = jnp.transpose(pair_label.reshape(2, 8, 2, 4, 2), (3, 0, 4, 1, 2)).reshape(16, 16).astype(F32)
    scal = jnp.broadcast_to(
        jnp.concatenate([logit_params, counts.reshape(1).astype(F32), jnp.zeros((5,), F32)])[:, None], (8, 128)
    )
    vm = pltpu.VMEM
    scratch = [
        vm((2, 8, 2, 4, 9, 32, 128), BF16),
        vm((2, 8, 2, 13, 32, 128), BF16),
        vm((D, D), BF16),
        vm((ROWS, D), F32),
        vm((ROWS, D), F32),
        vm((ROWS, 128), F32),
        vm((ROWS, D), BF16),
        vm((NT_IN, ROWS, 128), F32),
        vm((NT_IN, 1, 128), F32),
        vm((NT_IN, 1, 128), F32),
        vm((ROWS, D), F32),
        vm((NT_IN, 128, 128), BF16),
        vm((9, 128, 128), BF16),
        vm((1024, 1024), BF16),
        vm((8, D), F32),
        vm((1, D), F32),
        vm((16, 1, 1280), F32),
        vm((2, 16, 16, 640), BF16),
        vm((8, 5, 1, 128), F32),
        vm((8, 1, D), F32),
        vm((8, 1, D), F32),
        vm((8, 1, D), F32),
        vm((8, 5, 1, 128), F32),
        vm((8, 5, 1, 128), F32),
        vm((16, 1, 1280), F32),
        vm((16, 1, 1280), F32),
        vm((16, 1, 1280), F32),
        pltpu.SemaphoreType.DMA((N_COPIES,)),
        pltpu.SemaphoreType.DMA((N_COPIES,)),
    ]
    spec = pl.BlockSpec(memory_space=pltpu.VMEM)
    patch_grad, text_grad, stats = pl.pallas_call(
        kernel,
        out_shape=(
            jax.ShapeDtypeStruct((ROWS, D), BF16),
            jax.ShapeDtypeStruct((1, D), BF16),
            jax.ShapeDtypeStruct((1, 128), F32),
        ),
        in_specs=[spec] * 8,
        out_specs=(spec, spec, spec),
        scratch_shapes=scratch,
        compiler_params=pltpu.CompilerParams(
            collective_id=0, has_side_effects=True, vmem_limit_bytes=56 * 2**20
        ),
    )(rows, wi, wo, vec, bias, labels.reshape(1, 256), jnp.pad(labels, ((0, 0), (0, 112))), scal)
    return patch_grad.reshape(patches.shape), text_grad, stats[0, :3]


def solution(mesh):
    return jax.shard_map(
        shards,
        mesh=mesh,
        in_specs=(
            P("dp", "blk", None, None),
            P("dp", "blk", None),
            P(),
            P(),
            P("dp", None),
            P(),
            P(None, "dp"),
            P(),
            P(("dp", "blk"), None),
            P(),
            P(),
        ),
        out_specs=(P("dp", "blk", None, None), P(("dp", "blk"), None), P()),
        check_vma=False,
    )
```

time: 811 us -> 122 us (0.15)
  waiting for transfers between devices: 432 us -> 0 us
  blocking collectives: 181 us -> 0 us
  Pallas kernels: 0 us -> 108 us
  matrix products: 61.1 us -> 0 us
  other arithmetic: 43.9 us -> 0.76 us
  local copies, waits for them, and re-layouts: 49.8 us -> 11.3 us
  starting transfers between devices: 23.9 us -> 0 us
  between operations: 17 us -> 1.42 us
    unnamed x4 -> x0, waiting for transfers between devices: 243 us -> none
    all_gather x2 -> x0, waiting for transfers between devices: 155 us -> none  [the longest x1 89.5 us: shards(): lax.all_gather(weight_out, 'dp', axis=1, tiled=True)]
    pallas_call x0 -> x1, Pallas kernels: none -> 108 us  [shards(): pl.pallas_call(kernel, out_shape=(jax.ShapeDtypeStruct((ROWS, D), BF16),...]
    all_gather x2 -> x0, blocking collectives: 85.8 us -> none  [the longest x1 43.3 us: shards(): lax.all_gather(per_image, 'dp', axis=0, tiled=True)]
    psum x1 -> x0, blocking collectives: 76.3 us -> none  [shards(): statistics = lax.psum(loss_sums, ('dp', 'blk')) / pairs_total]
    dot_general x20 -> x0, matrix products: 61.1 us -> none  [the longest x9 39.6 us: contract_last(): lax.dot_general(left, right, (((1,), (1,)), ((), ())), preferred_element_...]
    unnamed x64 -> x19, local copies, waits for them, and re-layouts: 32.3 us -> 4.07 us
    add x25 -> x0, other arithmetic: 25.5 us -> none  [the longest x16 24.8 us: cycle_turn(): return (text_block, travel, image_acc + image_part, loss_sums + term_sums)]
  transfers between devices with their start and end apart: 22 -> 0, of which waited for: 12 -> 0; matrix products, arithmetic and copies ran while one was open for 12% -> 0% of each run, Pallas kernels for 0% -> 0%
where the time goes in v1:
time: 122 us; the launch traced here: 121 us
  Pallas kernels  108 us (89%)
  local copies, waits for them, and re-layouts  11.3 us (9%)
  between operations  1.42 us (1%)
    pallas_call x1, Pallas kernels, shards(): pl.pallas_call(kernel, out_shape=(jax.ShapeDtypeStruct((ROWS, D), BF16),...  108 us
    unnamed x19, local copies, waits for them, and re-layouts  4.07 us

profile of v1, /device:TPU:1, one launch (start us, length us, event | category | flops | bytes accessed | tf_op | source)
XLA Modules:
  0.0 121.5 jit_solution(7065281335413960200)
XLA Ops:
  0.6 0.7 convert_element_type.42
  1.3 0.2 convert_element_type.43
  1.5 0.5 copy.16
  2.0 0.1 convert_element_type.46
  2.1 0.6 pad.19.lab2_ref
  2.7 0.7 convert_element_type.45.labl_ref
  3.4 1.5 %copy.15 = bf16[4304,36]{1,0:T(8,128)(2,1)S(1)} copy(bf16[4304,36]{0,1:T(8,128)(2,1)} %param.17) | data formatting | bytes 619776 | tf_op args[6]
  4.9 0.0 copy-start
  4.9 0.0 copy-start.2
  4.9 0.0 copy-start.3
  4.9 0.0 copy-start.4
  4.9 0.0 copy-start.5
  5.0 0.0 copy-start.1
  5.0 0.0 copy-start.7
  5.0 1.2 %pad.17.wo_ref = bf16[4352,36]{1,0:T(8,128)(2,1)} pad(bf16[4304,36]{1,0:T(8,128)(2,1)S(1)} %copy.15, bf16[]{:T(256)} %constant.2.clone.1), padding=0_48x0_0 | pad | bytes 623234 | tf_op jit(solution)/shard_map/jit(_pad)/pad | solution.py:529
  6.2 0.0 copy-done
  6.2 0.8 pad.16.wi_ref
  7.0 0.0 copy-done.2
  7.0 0.0 copy-done.3
  7.0 0.0 copy-done.4
  7.0 0.0 copy-done.5
  7.0 0.7 concatenate.6.vec_ref
  7.7 0.0 copy-done.1
  7.7 0.6 reshape.36.bin_ref
  9.0 0.0 copy-done.7
  9.0 0.1 pad_maximum_fusion
  9.1 0.7 broadcast_in_dim.22.sc_ref
  9.7 108.0 %shard_map.130 = (bf16[256,1152]{1,0:T(8,128)(2,1)}, bf16[1,1152]{1,0:T(2,128)(2,1)}, f32[1,128]{1,0:T(1,128)}) custom-call(bf16[256,1152]{1,0:T(8,128)(2,1)} %bitcast.10, bf16[48,4352]{1,0:T(8,128)(2,1)} %pad.16.wi_ref, bf16[4352,36]{1,0:T(8,128)(2,1)} %pad.17.wo_ref, f32[8,1152]{1,0:T(8,128)} %concatenate.6.vec_ref, f32[34,1,128]{2,1,0:T(1,128)} %reshape.36.bin_ref, ...), custom_call_target="tpu_custom_call" | custom-call | tf_op jit(solution)/shard_map/pallas_call | solution.py:571
  117.8 0.0 copy-start.6
  117.8 1.2 slice_bitcast_fusion
  118.9 1.9 %copy.21 = bf16[1,1,256,1152]{3,2,1,0:T(8,128)(2,1)} copy(bf16[1,1,256,1152]{3,2,1,0:T(8,128)(2,1)} %bitcast.11) | data formatting | bytes 1179648
  120.9 0.0 copy-done.6
  120.9 0.6 copy.22
  (6 shorter events, 0.0 us)
Async XLA Ops:
  4.9 1.3 %copy-start = (bf16[36,4304]{1,0:T(8,128)(2,1)S(1)}, bf16[36,4304]{1,0:T(8,128)(2,1)}, u32[]{:S(2)}) copy-start(bf16[36,4304]{1,0:T(8,128)(2,1)} %param.15) | copy-start | bytes 929668
  4.9 2.1 %copy-start.2 = (f32[1152]{0:T(1024)S(1)}, f32[1152]{0:T(1024)}, u32[]{:S(2)}) copy-start(f32[1152]{0:T(1024)} %param.13) | copy-start | bytes 13828
  4.9 2.1 %copy-start.3 = (f32[1152]{0:T(1024)S(1)}, f32[1152]{0:T(1024)}, u32[]{:S(2)}) copy-start(f32[1152]{0:T(1024)} %param.14) | copy-start | bytes 13828
  4.9 2.1 %copy-start.4 = (f32[1152]{0:T(1024)S(1)}, f32[1152]{0:T(1024)}, u32[]{:S(2)}) copy-start(f32[1152]{0:T(1024)} %param.18) | copy-start | bytes 13828
  4.9 2.1 %copy-start.5 = (bf16[1,1152]{1,0:T(2,128)(2,1)S(1)}, bf16[1,1152]{1,0:T(2,128)(2,1)}, u32[]{:S(2)}) copy-start(bf16[1,1152]{1,0:T(2,128)(2,1)} %param.19) | copy-start | bytes 6916
  5.0 2.8 %copy-start.1 = (f32[4304]{0:T(1024)S(1)}, f32[4304]{0:T(1024)}, u32[]{:S(2)}) copy-start(f32[4304]{0:T(1024)} %param.16) | copy-start | bytes 51652
  5.0 4.0 %copy-start.7 = (f32[2]{0:T(128)S(1)}, f32[2]{0:T(128)}, u32[]{:S(2)}) copy-start(f32[2]{0:T(128)} %param.21) | copy-start | bytes 28
  117.8 3.1 %copy-start.6 = (bf16[1,1152]{1,0:T(2,128)(2,1)S(1)}, bf16[1,1152]{1,0:T(2,128)(2,1)}, u32[]{:S(2)}) copy-start(bf16[1,1152]{1,0:T(2,128)(2,1)} %get-tuple-element.13) | copy-start | bytes 6916

commit v2 on v1

--- a/solution.py
+++ b/solution.py
@@ -76,6 +76,7 @@
 
     bar = pltpu.get_barrier_semaphore()
     greet = col_devs + plane_devs + [dev(x + d, y, z, c + 1) for d in (1, 2, 3)]
+    greet += [dev(x, y + 3 + 2 * yl, z + d, c) for d in (1, 2, 6, 7)]
     for peer in greet:
         pl.semaphore_signal(bar, inc=1, device_id=peer, device_id_type=MESH)
 
@@ -110,8 +111,8 @@
     wi_tail = wi_ref[32:48, :].astype(F32)[0:8]
     for q in range(4):
         for t in range(8):
-            G[yh, z, c, q, 5 * (t // 4) + t % 4] = wi_ref[0:32, 1024 * q + 128 * t : 1024 * q + 128 * t + 128]
-        G[yh, z, c, q, 4] = fold(wi_tail, 8 * q, 8)
+            G[yh, 0, c, q, 5 * (t // 4) + t % 4] = wi_ref[0:32, 1024 * q + 128 * t : 1024 * q + 128 * t + 128]
+        G[yh, 0, c, q, 4] = fold(wi_tail, 8 * q, 8)
     eye = (
         lax.broadcasted_iota(jnp.int32, (48, 36), 0) == lax.broadcasted_iota(jnp.int32, (48, 36), 1)
     ).astype(F32).astype(BF16)
@@ -120,89 +121,21 @@
     wo_t = nt_dot(eye, wo_rows)
     wo_main = wo_t[0:32].astype(BF16)
     for t in range(2):
-        W[yh, z, c, t] = wi_ref[0:32, 4096 + 128 * t : 4096 + 128 * t + 128]
+        W[yh, 0, c, t] = wi_ref[0:32, 4096 + 128 * t : 4096 + 128 * t + 128]
     for t in range(9):
-        W[yh, z, c, 2 + t] = wo_main[:, 128 * t : 128 * t + 128]
+        W[yh, 0, c, 3 + t] = wo_main[:, 128 * t : 128 * t + 128]
     tail = jnp.concatenate([wi_tail[:, 4096:4352], wo_t[32:40]], axis=1)
-    W[yh, z, c, 11] = fold(tail, 0, 8)
-    W[yh, z, c, 12] = fold(tail, 8, 3)
-
-    pl.semaphore_wait(bar, len(greet))
-
-    def zz(d):
-        return (z + 8 + d) % 8
-
-    other = 1 - yh
-    both = slice(None)
-    mine5 = pl.ds(4 * yl, 5)
-    mine4 = pl.ds(5 * yl, 4)
-    pair0 = 2 * (x // 2)
-    pair1 = 2 - pair0
-
-    def z_in(n):
-        if n < 4:
-            got(("zR", n - 1))
-            got(("zL", n - 1))
-            if n == 1:
-                got(("zRb", 0))
-                got(("zLb", 0))
-            sel_r = both if n < 3 else 0
-            sel_l = both if n < 3 else 1
-            same(("zR", n), G.at[sel_r, zz(-n), c, x, mine5], zp)
-            same(("zL", n), G.at[sel_l, zz(n), c, x, mine5], zm)
-        else:
-            got(("zR", 3))
-            got(("zL", 3))
-
-    def d_in(n):
-        if n == 0:
-            got(("d1",))
-        else:
-            got(("dR", n - 1))
-            got(("dL", n - 1))
-        if n < 4:
-            sel_r = both if n < 3 else 0
-            sel_l = both if n < 3 else 1
-            same(("dR", n), W.at[sel_r, zz(-n), c], zp)
-            same(("dL", n), W.at[sel_l, zz(n), c], zm)
-
-    def d_partner(dz):
-        same(("pD", dz), W.at[:, zz(dz), c], partner)
-
-    def x_send(dz):
-        sel = other if dz == 0 else both
-        same(("xR", dz), G.at[sel, zz(dz), c, x, mine5], xp)
-        same(("xL", dz), G.at[sel, zz(dz), c, x, mine5], xm)
-
-    def x_in(dz):
-        got(("xR", dz))
-        got(("xL", dz))
-        same(("fR", dz), G.at[other if dz == 0 else 0, zz(dz), c, (x + 3) % 4, mine5], xp)
-        if dz != 0:
-            same(("fL", dz), G.at[1, zz(dz), c, (x + 1) % 4, mine5], xm)
-            same(("yC", dz), G.at[:, zz(dz), c, pl.ds(pair0, 2), mine4], cross)
-
-    def f_in(dz):
-        got(("fR", dz))
-        if dz != 0:
-            got(("fL", dz))
-        sel = other if dz == 0 else both
-        same(("yS", dz), G.at[sel, zz(dz), c, pl.ds(pair1, 2), mine4], share)
-
-    def y_in(dz):
-        got(("yC", dz))
-        got(("yS", dz))
-        same(("pG", dz), G.at[:, zz(dz), c], partner)
-
-    same(("e1",), G.at[yh, z, c, x, pl.ds(4 * (1 - yl), 5)], cross)
-    same(("zR", 0), G.at[yh, z, c, x, mine5], zp)
-    same(("zL", 0), G.at[yh, z, c, x, mine5], zm)
-    same(("yC", 0), G.at[yh, z, c, pl.ds(pair0, 2), mine4], cross)
-    same(("d1",), W.at[yh, z, c], cross)
+    W[yh, 0, c, 2] = fold(tail, 0, 8)
+    W[yh, 0, c, 12] = fold(tail, 8, 3)
 
     lane = lax.broadcasted_iota(jnp.int32, (1, D), 1)
     rest = lane - 1024
-    natural = jnp.where(lane < 1024, 36 * (lane >> 5) + (lane & 31), 36 * (rest >> 2) + 32 + (rest & 3))
+    place = jnp.where(lane < 1024, lane >> 5, rest >> 2)
+    row_in = jnp.where(lane < 1024, lane & 31, 32 + (rest & 3))
+    slot = (place >> 1) & 7
+    steps = ((slot + 1) >> 1) * (1 - 2 * (slot & 1))
+    shard = (place >> 4) * 16 + ((z + 8 + steps) & 7) * 2 + (place & 1)
+    natural = 36 * shard + row_in
 
     @pl.loop(0, 9)
     def _(i):
@@ -210,25 +143,14 @@
         rows = lax.broadcasted_iota(jnp.int32, (128, D), 0) + 128 * i
         PM[pl.ds(first, 128), :] = jnp.where(rows == natural, 1.0, 0.0).astype(BF16)
 
-    got(("e1",))
-    same(("zRb", 0), G.at[other, z, c, x, mine5], zp)
-    same(("zLb", 0), G.at[other, z, c, x, mine5], zm)
-    x_send(0)
-
-    VP[...] = exact_dot(vec_ref[...], PM[...], nn_dot)
-    gain, nbias, bout, text_f = VP[0:1, :], VP[1:2, :], VP[2:3, :], VP[3:4, :]
+    text_f = vec_ref[3:4, :]
     txt_norm = jnp.sqrt(jnp.sum(text_f * text_f, axis=1, keepdims=True) + NORM_EPS)
     txt_unit = text_f / txt_norm
     TROW[...] = txt_unit
     TCOL[u] = jnp.concatenate([txt_unit.astype(BF16).astype(F32), jnp.zeros((1, 128), F32)], axis=1)
-    for i, device in enumerate(col_devs):
-        same(("t1", i), TCOL.at[u], device)
-
-    z_in(1)
-    x_send(-1)
-    x_send(1)
-    x_in(0)
-
+
+    VP[...] = exact_dot(vec_ref[...], PM[...], nn_dot)
+    gain, nbias, bout = VP[0:1, :], VP[1:2, :], VP[2:3, :]
     count = sc_ref[2:3, 0:1]
 
     @pl.loop(0, 4)
@@ -243,43 +165,6 @@
         RSTD[rows, :] = jnp.broadcast_to(inv, (64, 128))
         NM[rows, :] = (plain * gain + nbias).astype(BF16)
 
-    f_in(0)
-    for i in range(15):
-        got(("t1", i))
-    block = TCOL[...].reshape(16, 1280).astype(BF16)
-    TB[c, v] = jnp.where(c == 0, block[:, :640].astype(F32), block[:, 640:].astype(F32)).astype(BF16)
-    for i, device in enumerate(plane_devs):
-        same(("t2", i), TB.at[c, v], device)
-
-    z_in(2)
-    x_send(-2)
-    x_send(2)
-    x_in(-1)
-    x_in(1)
-    y_in(0)
-    z_in(3)
-    x_send(-3)
-    x_send(3)
-    x_in(-2)
-    x_in(2)
-    f_in(-1)
-    f_in(1)
-    z_in(4)
-    x_send(4)
-    d_in(0)
-    y_in(-1)
-    y_in(1)
-    d_partner(0)
-    x_in(-3)
-    x_in(3)
-    f_in(-2)
-    f_in(2)
-    y_in(-2)
-    y_in(2)
-    for i in range(15):
-        got(("t2", i))
-    same(("t3",), TB.at[c], partner)
-
     row_ids = lax.broadcasted_iota(jnp.int32, (ROWS, 1), 0).astype(F32)
     valid = row_ids < count
     xsum = jnp.sum(jnp.where(valid, XP[...], 0.0), axis=0, keepdims=True)
@@ -292,30 +177,163 @@
             col == 32 * (r >> 2) + 4 * i + (r & 3), 1.0, 0.0
         ).astype(BF16)
 
+    pl.semaphore_wait(bar, len(greet))
+
+    other = 1 - yh
+    both = slice(None)
+    mine5 = pl.ds(4 * yl, 5)
+    mine4 = pl.ds(5 * yl, 4)
+    slots = [0, pl.ds(1, 2), pl.ds(3, 2), pl.ds(5, 2), 7]
+
+    zpp, zmm = dev(x, y, z + 2, c), dev(x, y, z + 6, c)
+    other5 = pl.ds(4 * (1 - yl), 5)
+
+    def z_own(k, device, over):
+        send(("zA", k), G.at[yh, 0, c, x, mine5], G.at[yh, k, c, x, mine5], device)
+        send(("zB", k), G.at[yh, 0, c, x, other5], G.at[yh, k, c, x, other5], over)
+
+    def z_forward():
+        for a in (0, 1):
+            send(("zF", 5, a), G.at[a, 3, c, x, mine5], G.at[a, 5, c, x, mine5], zp)
+            send(("zF", 6, a), G.at[a, 4, c, x, mine5], G.at[a, 6, c, x, mine5], zm)
+        send(("zF", 7), G.at[0, 3, c, x, mine5], G.at[0, 7, c, x, mine5], zpp)
+        send(("zF", 8), G.at[1, 4, c, x, mine5], G.at[1, 7, c, x, mine5], zmm)
+
+    chain_r, chain_l = (0, 1, 3, 5, 7), (0, 2, 4, 6, 7)
+
+    part_in, part_out = pl.ds(0, 3), pl.ds(3, 10)
+
+    def w_send(name, sel, src, dst, tiles, device):
+        send(name, W.at[sel, src, c, tiles], W.at[sel, dst, c, tiles], device)
+
+    def di_send(n):
+        w_send(("iR", n), both if n < 3 else 0, chain_r[n], chain_r[n + 1], part_in, zp)
+        w_send(("iL", n), both if n < 3 else 1, chain_l[n], chain_l[n + 1], part_in, zm)
+
+    def di_in(n):
+        got(("iR", n - 1))
+        got(("iL", n - 1))
+        if n < 4:
+            di_send(n)
+
+    def d_send(n, a, sel):
+        if n < 3 or a == 0:
+            w_send(("dR", n, a), sel, chain_r[n], chain_r[n + 1], part_out, zp)
+        if n < 3 or a == 1:
+            w_send(("dL", n, a), sel, chain_l[n], chain_l[n + 1], part_out, zm)
+
+    def d_in(n, a):
+        if n < 4 or a == 0:
+            got(("dR", n - 1, a))
+        if n < 4 or a == 1:
+            got(("dL", n - 1, a))
+        if n < 4:
+            d_send(n, a, yh if a == 0 else other)
+
+    def d_partner(n):
+        same(("pD", n), W.at[:, slots[n], c, part_out], partner)
+
+    def y_send(name, sel, g, q, device):
+        same((name, g), G.at[sel, slots[g], c, q % 4, mine4], device)
+
+    def x_send(g):
+        sel = other if g == 0 else both
+        same(("xR", g), G.at[sel, slots[g], c, x, mine5], xp)
+        same(("xL", g), G.at[sel, slots[g], c, x, mine5], xm)
+        if g != 0:
+            y_send("yA", both, g, x, cross)
+
+    def x_in(g):
+        got(("xR", g))
+        got(("xL", g))
+        sel = other if g == 0 else both
+        same(("fR", g), G.at[other if g == 0 else 0, slots[g], c, (x + 3) % 4, mine5], xp)
+        if g != 0:
+            same(("fL", g), G.at[1, slots[g], c, (x + 1) % 4, mine5], xm)
+        y_send("yB", sel, g, x + 3, share)
+        y_send("yC", sel, g, x + 1, share)
+
+    def f_in(g):
+        got(("fR", g))
+        if g != 0:
+            got(("fL", g))
+            y_send("yD", both, g, x + 2, cross)
+
+    def y_in(g):
+        for name in ("yA", "yB", "yC", "yD"):
+            got((name, g))
+        same(("pG", g), G.at[:, slots[g], c], partner)
+
+    yc = y + 3 + 2 * yl
+    z_own(1, zp, dev(x, yc, z + 1, c))
+    z_own(2, zm, dev(x, yc, z + 7, c))
+    same(("e1",), G.at[yh, 0, c, x, other5], cross)
+    z_own(3, zpp, dev(x, yc, z + 2, c))
+    z_own(4, zmm, dev(x, yc, z + 6, c))
+    same(("i1",), W.at[yh, 0, c, part_in], cross)
+    y_send("yA", yh, 0, x, cross)
+    y_send("yD", yh, 0, x + 2, cross)
+    for i, device in enumerate(col_devs):
+        same(("t1", i), TCOL.at[u], device)
+    got(("e1",))
+    x_send(0)
+    got(("i1",))
+    for k in (1, 2):
+        got(("zA", k))
+        got(("zB", k))
+    x_send(1)
+    for k in (3, 4):
+        got(("zA", k))
+        got(("zB", k))
+    z_forward()
+    x_send(2)
+    di_send(0)
+    same(("d1",), W.at[yh, 0, c, part_out], cross)
+    d_send(0, 0, yh)
+    x_in(0)
+    x_in(1)
+    for k in (5, 6):
+        for a in (0, 1):
+            got(("zF", k, a))
+    x_send(3)
+    for k in (7, 8):
+        got(("zF", k))
+    x_send(4)
+    di_in(1)
+    got(("d1",))
+    d_send(0, 1, other)
+    x_in(2)
+    f_in(0)
+    f_in(1)
+    d_in(1, 0)
+    di_in(2)
+    y_in(0)
+    x_in(3)
+    f_in(2)
     x_in(4)
-    f_in(-3)
+    d_in(1, 1)
+    di_in(3)
+    y_in(1)
     f_in(3)
-    d_in(1)
-    d_partner(-1)
-    d_partner(1)
-    y_in(-3)
+    d_in(2, 0)
+    f_in(4)
+    y_in(2)
+    di_in(4)
+    same(("pI",), W.at[:, :, c, part_in], partner)
+    d_in(2, 1)
+    for i in range(15):
+        got(("t1", i))
+    block = TCOL[...].reshape(16, 1280).astype(BF16)
+    TB[c, v] = jnp.where(c == 0, block[:, :640].astype(F32), block[:, 640:].astype(F32)).astype(BF16)
     y_in(3)
-    f_in(4)
-    d_in(2)
-    d_partner(-2)
-    d_partner(2)
     y_in(4)
-    d_in(3)
-    d_partner(-3)
-    d_partner(3)
-    d_in(4)
-    d_partner(4)
-    order = (0, -1, 1, -2, 2, -3, 3, 4)
-    for dz in order:
-        got(("pG", dz))
-    for dz in order:
-        got(("pD", dz))
-    got(("t3",))
+    for g in range(3):
+        d_partner(g)
+    for i, device in enumerate(plane_devs):
+        same(("t2", i), TB.at[c, v], device)
+    for g in range(5):
+        got(("pG", g))
+    got(("pI",))
 
     def unfold(store, pieces):
         res = nn_dot(SF[...], jnp.concatenate([p.reshape(1024, 128) for p in pieces], axis=1)).astype(BF16)
@@ -328,8 +346,8 @@
             RW[8 * (base + j) + a] = tile
         return store
 
-    def store_direct(j, a, tile):
-        t = 8 * j + a
+    def store_direct(j, a, tile, first=0):
+        t = first + a
         if t < 2:
             RW[32 + t] = tile
         elif t < 11:
@@ -337,7 +355,7 @@
 
     for q in (0, 2):
         unfold(store_in(q), [G[:, :, :, q, 4], G[:, :, :, q + 1, 4]])
-    unfold(store_direct, [W[:, :, :, 11], W[:, :, :, 12]])
+    unfold(store_direct, [W[:, :, :, 2]])
 
     def fwd(first, count_tiles, main_tiles):
         wm = jnp.concatenate([m.reshape(1024, 128) for m in main_tiles], axis=1)
@@ -352,16 +370,33 @@
             SL[first + t] = half + 0.5 * pre * (1.0 - th * th) * (GELU_SCALE + 3.0 * GELU_SCALE * GELU_CUBIC * sq)
             HS[first + t] = jnp.sum(jnp.where(valid, hid, 0.0), axis=0, keepdims=True)
 
-    @pl.loop(0, 8)
-    def _(p):
-        q, half = p // 2, p % 2
-        fwd(4 * p, 4, [G[:, :, :, q, 5 * half + t] for t in range(4)])
+    def fwd_pair(start):
+        @pl.loop(start, start + 2)
+        def _(p):
+            q, half = p // 2, p % 2
+            fwd(4 * p, 4, [G[:, :, :, q, 5 * half + t] for t in range(4)])
 
     fwd(32, 2, [W[:, :, :, 0], W[:, :, :, 1]])
-
+    d_in(3, 0)
+    fwd_pair(0)
+    d_in(3, 1)
+    d_partner(3)
+    fwd_pair(2)
+    d_in(4, 0)
+    fwd_pair(4)
+    d_in(4, 1)
+    d_partner(4)
+    fwd_pair(6)
+
+    for g in range(5):
+        got(("pD", g))
+    unfold(lambda j, a, tile: store_direct(j, a, tile, 8), [W[:, :, :, 12]])
     def first_tile(member):
         return 4 * member + member // 4
 
+    for i in range(15):
+        got(("t2", i))
+    same(("t3",), TB.at[c], partner)
     for i, (p, device) in enumerate(zip(ring_peers, ring_devs)):
         send(("h", i), HS.at[pl.ds(first_tile(p), 5)], HA.at[s], device)
     HA[s] = HS[pl.ds(first_tile(s), 5)]
@@ -375,7 +410,7 @@
         if t == 4:
             col = col * last_mine
         lhs = jnp.concatenate(split3(col), axis=0)
-        part_m += nt_dot(lhs, W[:, :, :, 2 + 4 * c + t].reshape(1024, 128))
+        part_m += nt_dot(lhs, W[:, :, :, 3 + 4 * c + t].reshape(1024, 128))
         part_r += nt_dot(lhs, RO[4 * c + t])
     part = jnp.concatenate([part_m, part_r], axis=1)
     part = part[0:8] + part[8:16] + part[16:24]
@@ -389,13 +424,14 @@
     mixed = jnp.sum(PR[...].reshape(8, D), axis=0, keepdims=True)
     pooled = (xsum + mixed) / count + bout
 
+    got(("t3",))
+    texts_nat = jnp.concatenate([TB[0].reshape(256, 640), TB[1].reshape(256, 640)[:, :512]], axis=1)
+    texts = nn_dot(texts_nat, PM[...]).astype(BF16)
     img_norm = jnp.sqrt(jnp.sum(pooled * pooled, axis=1, keepdims=True) + NORM_EPS)
     img_unit = pooled / img_norm
     img_b = img_unit.astype(BF16)
     scale = jnp.exp(sc_ref[0:1, 0:1])
     shift = sc_ref[1:2, 0:1]
-    texts = jnp.concatenate([TB[0].reshape(256, 640), TB[1].reshape(256, 640)[:, :512]], axis=1)
-
     def terms(inner, same_label):
         logits = scale * inner + shift
         sign = jnp.where(same_label, 1.0, -1.0)
@@ -403,7 +439,9 @@
         soft = jnp.maximum(neg, 0.0) + jnp.log1p(jnp.exp(-jnp.abs(neg)))
         return soft, -sign / (1.0 + jnp.exp(-neg))
 
-    inner = nt_dot(jnp.broadcast_to(img_b.astype(F32), (16, D)).astype(BF16), texts)[0:8]
+    img_rows = jnp.broadcast_to(img_b.astype(F32), (16, D)).astype(BF16)
+    inner = nt_dot(img_rows, texts)[0:8]
+    img_nat = nt_dot(img_rows, PM[...])[0:1]
     labels = labl_ref[...]
     lane256 = lax.broadcasted_iota(jnp.int32, (1, 256), 1)
     own_label = jnp.sum(jnp.where(lane256 == v * 16 + u, labels, 0.0), axis=1, keepdims=True)
@@ -415,7 +453,7 @@
     ]
     lane128 = lax.broadcasted_iota(jnp.int32, (1, 128), 1)
     stat_row = sum(jnp.where(lane128 == k, stats[k], 0.0) for k in range(3))
-    ICOL[u] = jnp.concatenate([img_b.astype(F32), stat_row], axis=1)
+    ICOL[u] = jnp.concatenate([img_nat, stat_row], axis=1)
     for i, device in enumerate(col_devs):
         same(("i1", i), ICOL.at[u], device)
 
@@ -430,7 +468,7 @@
         got(("g", i))
     grads = GB[...].reshape(8, D).astype(BF16)
     for t in range(5):
-        res = nn_dot(grads[:, :1024], W[:, :, :, 2 + 4 * c + t].reshape(1024, 128)) + nn_dot(
+        res = nn_dot(grads[:, :1024], W[:, :, :, 3 + 4 * c + t].reshape(1024, 128)) + nn_dot(
             grads[:, 1024:], RO[4 * c + t]
         )
         for j in range(8):
@@ -446,7 +484,7 @@
     pick = (
         lax.broadcasted_iota(jnp.int32, (16, 256), 1) == 16 * lax.broadcasted_iota(jnp.int32, (16, 256), 0) + u
     )
-    texts16 = nn_dot(jnp.where(pick, 1.0, 0.0).astype(BF16), texts).astype(BF16)
+    texts16 = nn_dot(jnp.where(pick, 1.0, 0.0).astype(BF16), texts_nat).astype(BF16)
     lab2 = lab2_ref[...]
     lab_txt = jnp.sum(
         jnp.where(lax.broadcasted_iota(jnp.int32, (16, 128), 1) == u, lab2, 0.0), axis=1, keepdims=True
@@ -512,9 +550,9 @@
     d_txt = scale * sums[:, :D]
     unit = TROW[...]
     tg = (d_txt - unit * jnp.sum(unit * d_txt, axis=1, keepdims=True)) / jnp.sqrt(
-        jnp.sum(VP[3:4, :] * VP[3:4, :], axis=1, keepdims=True) + NORM_EPS
+        jnp.sum(vec_ref[3:4, :] * vec_ref[3:4, :], axis=1, keepdims=True) + NORM_EPS
     )
-    tg_ref[...] = nt_dot(jnp.broadcast_to(tg, (16, D)).astype(BF16), PM[...])[0:1].astype(BF16)
+    tg_ref[...] = tg.astype(BF16)
 
     for cp in copies.values():
         cp.wait_send()

time: 122 us -> 104 us (0.85)
  Pallas kernels: 108 us -> 90.2 us
    pallas_call x1, Pallas kernels: 108 us -> 90.2 us  [shards(): pl.pallas_call(kernel, out_shape=(jax.ShapeDtypeStruct((ROWS, D), BF16),...]
where the time goes in v2:
time: 104 us
  Pallas kernels  90.2 us (87%)
  local copies, waits for them, and re-layouts  11.3 us (11%)
  between operations  1.42 us (1%)
    pallas_call x1, Pallas kernels, shards(): pl.pallas_call(kernel, out_shape=(jax.ShapeDtypeStruct((ROWS, D), BF16),...  90.2 us
    unnamed x19, local copies, waits for them, and re-layouts  4.07 us

profile of v2, /device:TPU:1, one launch (start us, length us, event | category | flops | bytes accessed | tf_op | source)
XLA Modules:
  0.0 103.7 jit_solution(13667076916103288848)
XLA Ops:
  0.6 0.7 convert_element_type.42
  1.3 0.2 convert_element_type.43
  1.5 0.5 copy.16
  2.0 0.1 convert_element_type.46
  2.1 0.6 pad.19.lab2_ref
  2.7 0.7 convert_element_type.45.labl_ref
  3.4 1.5 %copy.15 = bf16[4304,36]{1,0:T(8,128)(2,1)S(1)} copy(bf16[4304,36]{0,1:T(8,128)(2,1)} %param.17) | data formatting | bytes 619776 | tf_op args[6]
  4.9 0.0 copy-start
  4.9 0.0 copy-start.2
  4.9 0.0 copy-start.3
  4.9 0.0 copy-start.4
  4.9 0.0 copy-start.5
  5.0 0.0 copy-start.1
  5.0 0.0 copy-start.7
  5.0 1.2 %pad.17.wo_ref = bf16[4352,36]{1,0:T(8,128)(2,1)} pad(bf16[4304,36]{1,0:T(8,128)(2,1)S(1)} %copy.15, bf16[]{:T(256)} %constant.2.clone.1), padding=0_48x0_0 | pad | bytes 623234 | tf_op jit(solution)/shard_map/jit(_pad)/pad | solution.py:567
  6.2 0.0 copy-done
  6.2 0.8 pad.16.wi_ref
  7.0 0.0 copy-done.2
  7.0 0.0 copy-done.3
  7.0 0.0 copy-done.4
  7.0 0.0 copy-done.5
  7.0 0.7 concatenate.6.vec_ref
  7.7 0.0 copy-done.1
  7.7 0.6 reshape.36.bin_ref
  9.0 0.0 copy-done.7
  9.0 0.1 pad_maximum_fusion
  9.1 0.7 broadcast_in_dim.22.sc_ref
  9.7 90.2 %shard_map.130 = (bf16[256,1152]{1,0:T(8,128)(2,1)}, bf16[1,1152]{1,0:T(2,128)(2,1)}, f32[1,128]{1,0:T(1,128)}) custom-call(bf16[256,1152]{1,0:T(8,128)(2,1)} %bitcast.10, bf16[48,4352]{1,0:T(8,128)(2,1)} %pad.16.wi_ref, bf16[4352,36]{1,0:T(8,128)(2,1)} %pad.17.wo_ref, f32[8,1152]{1,0:T(8,128)} %concatenate.6.vec_ref, f32[34,1,128]{2,1,0:T(1,128)} %reshape.36.bin_ref, ...), custom_call_target="tpu_custom_call" | custom-call | tf_op jit(solution)/shard_map/pallas_call | solution.py:609
  100.0 0.0 copy-start.6
  100.0 1.2 %slice_bitcast_fusion = f32[3]{0:T(128)} fusion(f32[1,128]{1,0:T(1,128)} %get-tuple-element.8), kind=kLoop, calls=%fused_computation.1 | loop fusion | bytes 24 | tf_op jit(solution)/shard_map/squeeze | solution.py:623
  101.2 1.9 %copy.21 = bf16[1,1,256,1152]{3,2,1,0:T(8,128)(2,1)} copy(bf16[1,1,256,1152]{3,2,1,0:T(8,128)(2,1)} %bitcast.11) | data formatting | bytes 1179648
  103.1 0.0 copy-done.6
  103.1 0.6 copy.22
  (6 shorter events, 0.0 us)
Async XLA Ops:
  4.9 1.3 %copy-start = (bf16[36,4304]{1,0:T(8,128)(2,1)S(1)}, bf16[36,4304]{1,0:T(8,128)(2,1)}, u32[]{:S(2)}) copy-start(bf16[36,4304]{1,0:T(8,128)(2,1)} %param.15) | copy-start | bytes 929668
  4.9 2.1 %copy-start.2 = (f32[1152]{0:T(1024)S(1)}, f32[1152]{0:T(1024)}, u32[]{:S(2)}) copy-start(f32[1152]{0:T(1024)} %param.13) | copy-start | bytes 13828
  4.9 2.1 %copy-start.3 = (f32[1152]{0:T(1024)S(1)}, f32[1152]{0:T(1024)}, u32[]{:S(2)}) copy-start(f32[1152]{0:T(1024)} %param.14) | copy-start | bytes 13828
  4.9 2.1 %copy-start.4 = (f32[1152]{0:T(1024)S(1)}, f32[1152]{0:T(1024)}, u32[]{:S(2)}) copy-start(f32[1152]{0:T(1024)} %param.18) | copy-start | bytes 13828
  4.9 2.1 %copy-start.5 = (bf16[1,1152]{1,0:T(2,128)(2,1)S(1)}, bf16[1,1152]{1,0:T(2,128)(2,1)}, u32[]{:S(2)}) copy-start(bf16[1,1152]{1,0:T(2,128)(2,1)} %param.19) | copy-start | bytes 6916
  5.0 2.8 %copy-start.1 = (f32[4304]{0:T(1024)S(1)}, f32[4304]{0:T(1024)}, u32[]{:S(2)}) copy-start(f32[4304]{0:T(1024)} %param.16) | copy-start | bytes 51652
  5.0 4.0 %copy-start.7 = (f32[2]{0:T(128)S(1)}, f32[2]{0:T(128)}, u32[]{:S(2)}) copy-start(f32[2]{0:T(128)} %param.21) | copy-start | bytes 28
  100.0 3.1 %copy-start.6 = (bf16[1,1152]{1,0:T(2,128)(2,1)S(1)}, bf16[1,1152]{1,0:T(2,128)(2,1)}, u32[]{:S(2)}) copy-start(bf16[1,1152]{1,0:T(2,128)(2,1)} %get-tuple-element.13) | copy-start | bytes 6916

commit v3 on v2

--- a/solution.py
+++ b/solution.py
@@ -15,7 +15,7 @@
 F32 = jnp.float32
 BF16 = jnp.bfloat16
 NT_IN = 34
-N_COPIES = 180
+N_COPIES = 240
 
 
 def dev(x, y, z, c):
@@ -51,10 +51,11 @@
 
 
 def kernel(
-    x_ref, wi_ref, wo_ref, vec_ref, bin_ref, labl_ref, lab2_ref, sc_ref,
+    x_ref, wi_in, wo_in, vec_in, text_in, lab_in, lp_ref, cnt_ref,
     out_ref, tg_ref, st_ref,
     G, W, PM, XP, PLAIN, RSTD, NM, SL, HS, AF, ACC, RW, RO, SF, VP,
     TROW, TCOL, TB, HA, PB, PR, GB, AB, AR, ICOL, DB, DT,
+    WS, BS, VEC,
     SS, RS,
 ):
     dp, blk = lax.axis_index("dp"), lax.axis_index("blk")
@@ -108,74 +109,35 @@
             parts.append(sum(blocks) if blocks else jnp.zeros((8, 128), F32))
         return jnp.concatenate(parts, axis=0).astype(BF16)
 
+    for k, w_ref in ((0, wi_in), (1, wo_in)):
+        WS[k, :, 4224:4352] = jnp.zeros((48, 128), BF16)
+        WS[k, 32:48, :] = jnp.zeros((16, 4352), BF16)
+        WS[k, 0:32, 0:FF] = w_ref[0:32, :]
+        WS[k, 32:36, 0:FF] = w_ref[32:36, :]
+    wi_ref, wo_ref = WS.at[0], WS.at[1]
+    BS[:, 4224:4352] = jnp.zeros((1, 128), F32)
+    BS[:, 0:FF] = vec_in[:, 3 * D :]
+    VEC[...] = jnp.zeros((8, D), F32)
+    VEC[0:1, :] = vec_in[:, 0 * D : 1 * D]
+    VEC[1:2, :] = vec_in[:, 1 * D : 2 * D]
+    VEC[2:3, :] = vec_in[:, 2 * D : 3 * D]
+    VEC[3:4, :] = text_in[...].astype(F32)
     wi_tail = wi_ref[32:48, :].astype(F32)[0:8]
     for q in range(4):
         for t in range(8):
             G[yh, 0, c, q, 5 * (t // 4) + t % 4] = wi_ref[0:32, 1024 * q + 128 * t : 1024 * q + 128 * t + 128]
         G[yh, 0, c, q, 4] = fold(wi_tail, 8 * q, 8)
-    eye = (
-        lax.broadcasted_iota(jnp.int32, (48, 36), 0) == lax.broadcasted_iota(jnp.int32, (48, 36), 1)
-    ).astype(F32).astype(BF16)
     wo_first = 8 * x + x // 2
-    wo_rows = wo_ref[pl.ds(pl.multiple_of(128 * wo_first, 128), 1152), :]
-    wo_t = nt_dot(eye, wo_rows)
-    wo_main = wo_t[0:32].astype(BF16)
+    wo_cols = pl.ds(pl.multiple_of(128 * wo_first, 128), 1152)
+    wo_main = wo_ref[0:32, wo_cols]
+    wo_tail = wo_ref[32:48, wo_cols].astype(F32)[0:8]
     for t in range(2):
         W[yh, 0, c, t] = wi_ref[0:32, 4096 + 128 * t : 4096 + 128 * t + 128]
     for t in range(9):
         W[yh, 0, c, 3 + t] = wo_main[:, 128 * t : 128 * t + 128]
-    tail = jnp.concatenate([wi_tail[:, 4096:4352], wo_t[32:40]], axis=1)
+    tail = jnp.concatenate([wi_tail[:, 4096:4352], wo_tail], axis=1)
     W[yh, 0, c, 2] = fold(tail, 0, 8)
     W[yh, 0, c, 12] = fold(tail, 8, 3)
-
-    lane = lax.broadcasted_iota(jnp.int32, (1, D), 1)
-    rest = lane - 1024
-    place = jnp.where(lane < 1024, lane >> 5, rest >> 2)
-    row_in = jnp.where(lane < 1024, lane & 31, 32 + (rest & 3))
-    slot = (place >> 1) & 7
-    steps = ((slot + 1) >> 1) * (1 - 2 * (slot & 1))
-    shard = (place >> 4) * 16 + ((z + 8 + steps) & 7) * 2 + (place & 1)
-    natural = 36 * shard + row_in
-
-    @pl.loop(0, 9)
-    def _(i):
-        first = pl.multiple_of(128 * i, 128)
-        rows = lax.broadcasted_iota(jnp.int32, (128, D), 0) + 128 * i
-        PM[pl.ds(first, 128), :] = jnp.where(rows == natural, 1.0, 0.0).astype(BF16)
-
-    text_f = vec_ref[3:4, :]
-    txt_norm = jnp.sqrt(jnp.sum(text_f * text_f, axis=1, keepdims=True) + NORM_EPS)
-    txt_unit = text_f / txt_norm
-    TROW[...] = txt_unit
-    TCOL[u] = jnp.concatenate([txt_unit.astype(BF16).astype(F32), jnp.zeros((1, 128), F32)], axis=1)
-
-    VP[...] = exact_dot(vec_ref[...], PM[...], nn_dot)
-    gain, nbias, bout = VP[0:1, :], VP[1:2, :], VP[2:3, :]
-    count = sc_ref[2:3, 0:1]
-
-    @pl.loop(0, 4)
-    def _(i):
-        rows = pl.ds(pl.multiple_of(64 * i, 64), 64)
-        xs = nn_dot(x_ref[rows, :], PM[...])
-        XP[rows, :] = xs
-        centre = xs - jnp.mean(xs, axis=1, keepdims=True)
-        inv = lax.rsqrt(jnp.mean(centre * centre, axis=1, keepdims=True) + NORM_EPS)
-        plain = centre * inv
-        PLAIN[rows, :] = plain
-        RSTD[rows, :] = jnp.broadcast_to(inv, (64, 128))
-        NM[rows, :] = (plain * gain + nbias).astype(BF16)
-
-    row_ids = lax.broadcasted_iota(jnp.int32, (ROWS, 1), 0).astype(F32)
-    valid = row_ids < count
-    xsum = jnp.sum(jnp.where(valid, XP[...], 0.0), axis=0, keepdims=True)
-
-    @pl.loop(0, 8)
-    def _(i):
-        r = lax.broadcasted_iota(jnp.int32, (128, 1024), 0)
-        col = lax.broadcasted_iota(jnp.int32, (128, 1024), 1)
-        SF[pl.ds(pl.multiple_of(128 * i, 128), 128), :] = jnp.where(
-            col == 32 * (r >> 2) + 4 * i + (r & 3), 1.0, 0.0
-        ).astype(BF16)
 
     pl.semaphore_wait(bar, len(greet))
 
@@ -258,26 +220,52 @@
         if g != 0:
             got(("fL", g))
             y_send("yD", both, g, x + 2, cross)
+        same(("pF", g), G.at[:, slots[g], c, :, mine5], partner)
 
     def y_in(g):
         for name in ("yA", "yB", "yC", "yD"):
             got((name, g))
-        same(("pG", g), G.at[:, slots[g], c], partner)
+        same(("pG", g), G.at[:, slots[g], c, :, pl.ds(5 * (1 - yl), 4)], partner)
 
     yc = y + 3 + 2 * yl
     z_own(1, zp, dev(x, yc, z + 1, c))
     z_own(2, zm, dev(x, yc, z + 7, c))
     same(("e1",), G.at[yh, 0, c, x, other5], cross)
+    text_f = VEC[3:4, :]
+    txt_norm = jnp.sqrt(jnp.sum(text_f * text_f, axis=1, keepdims=True) + NORM_EPS)
+    txt_unit = text_f / txt_norm
+    TROW[...] = txt_unit
+    TCOL[u] = jnp.concatenate([txt_unit.astype(BF16).astype(F32), jnp.zeros((1, 128), F32)], axis=1)
+
+    for i, device in enumerate(col_devs):
+        same(("t1", i), TCOL.at[u], device)
     z_own(3, zpp, dev(x, yc, z + 2, c))
     z_own(4, zmm, dev(x, yc, z + 6, c))
     same(("i1",), W.at[yh, 0, c, part_in], cross)
     y_send("yA", yh, 0, x, cross)
     y_send("yD", yh, 0, x + 2, cross)
-    for i, device in enumerate(col_devs):
-        same(("t1", i), TCOL.at[u], device)
+    lane = lax.broadcasted_iota(jnp.int32, (1, D), 1)
+    rest = lane - 1024
+    place = jnp.where(lane < 1024, lane >> 5, rest >> 2)
+    row_in = jnp.where(lane < 1024, lane & 31, 32 + (rest & 3))
+    slot = (place >> 1) & 7
+    steps = ((slot + 1) >> 1) * (1 - 2 * (slot & 1))
+    shard = (place >> 4) * 16 + ((z + 8 + steps) & 7) * 2 + (place & 1)
+    natural = 36 * shard + row_in
+
+    @pl.loop(0, 9)
+    def _(i):
+        first = pl.multiple_of(128 * i, 128)
+        rows = lax.broadcasted_iota(jnp.int32, (128, D), 0) + 128 * i
+        PM[pl.ds(first, 128), :] = jnp.where(rows == natural, 1.0, 0.0).astype(BF16)
+
     got(("e1",))
     x_send(0)
     got(("i1",))
+    VP[...] = exact_dot(VEC[...], PM[...], nn_dot)
+    gain, nbias, bout = VP[0:1, :], VP[1:2, :], VP[2:3, :]
+    count = jnp.zeros((1, 128), F32)[:, 0:1] + cnt_ref[0].astype(F32)
+
     for k in (1, 2):
         got(("zA", k))
         got(("zB", k))
@@ -291,6 +279,18 @@
     same(("d1",), W.at[yh, 0, c, part_out], cross)
     d_send(0, 0, yh)
     x_in(0)
+    @pl.loop(0, 4)
+    def _(i):
+        rows = pl.ds(pl.multiple_of(64 * i, 64), 64)
+        xs = nn_dot(x_ref[rows, :], PM[...])
+        XP[rows, :] = xs
+        centre = xs - jnp.mean(xs, axis=1, keepdims=True)
+        inv = lax.rsqrt(jnp.mean(centre * centre, axis=1, keepdims=True) + NORM_EPS)
+        plain = centre * inv
+        PLAIN[rows, :] = plain
+        RSTD[rows, :] = jnp.broadcast_to(inv, (64, 128))
+        NM[rows, :] = (plain * gain + nbias).astype(BF16)
+
     x_in(1)
     for k in (5, 6):
         for a in (0, 1):
@@ -300,6 +300,10 @@
         got(("zF", k))
     x_send(4)
     di_in(1)
+    row_ids = lax.broadcasted_iota(jnp.int32, (ROWS, 1), 0).astype(F32)
+    valid = row_ids < count
+    xsum = jnp.sum(jnp.where(valid, XP[...], 0.0), axis=0, keepdims=True)
+
     got(("d1",))
     d_send(0, 1, other)
     x_in(2)
@@ -308,12 +312,37 @@
     d_in(1, 0)
     di_in(2)
     y_in(0)
+    @pl.loop(0, 8)
+    def _(i):
+        r = lax.broadcasted_iota(jnp.int32, (128, 1024), 0)
+        col = lax.broadcasted_iota(jnp.int32, (128, 1024), 1)
+        SF[pl.ds(pl.multiple_of(128 * i, 128), 128), :] = jnp.where(
+            col == 32 * (r >> 2) + 4 * i + (r & 3), 1.0, 0.0
+        ).astype(BF16)
+
     x_in(3)
     f_in(2)
     x_in(4)
     d_in(1, 1)
     di_in(3)
     y_in(1)
+    labels_nat = jnp.broadcast_to(lab_in[...].astype(F32), (16, 256))
+
+    def natural_pair(v_, u_):
+        return ((((v_ >> 1) & 1) * 16 + u_) * 8) + ((v_ >> 2) * 2) + (v_ & 1)
+
+    row256 = lax.broadcasted_iota(jnp.int32, (256, 256), 0)
+    col256 = lax.broadcasted_iota(jnp.int32, (256, 256), 1)
+    labels_b = labels_nat.astype(BF16)
+    labels = nn_dot(labels_b, jnp.where(row256 == natural_pair(col256 >> 4, col256 & 15), 1.0, 0.0).astype(BF16))[0:1]
+    own_label = jnp.sum(jnp.where(col256[0:1] == v * 16 + u, labels, 0.0), axis=1, keepdims=True)
+    lab_img = nn_dot(
+        labels_b, jnp.where(row256[:, :128] == natural_pair(v, col256[:, :128] & 15), 1.0, 0.0).astype(BF16)
+    )[0:1, :16]
+    lab_txt = jnp.sum(
+        jnp.where(col256[:16] == natural_pair(row256[:16], u), labels_nat, 0.0), axis=1, keepdims=True
+    )
+
     f_in(3)
     d_in(2, 0)
     f_in(4)
@@ -325,16 +354,6 @@
         got(("t1", i))
     block = TCOL[...].reshape(16, 1280).astype(BF16)
     TB[c, v] = jnp.where(c == 0, block[:, :640].astype(F32), block[:, 640:].astype(F32)).astype(BF16)
-    y_in(3)
-    y_in(4)
-    for g in range(3):
-        d_partner(g)
-    for i, device in enumerate(plane_devs):
-        same(("t2", i), TB.at[c, v], device)
-    for g in range(5):
-        got(("pG", g))
-    got(("pI",))
-
     def unfold(store, pieces):
         res = nn_dot(SF[...], jnp.concatenate([p.reshape(1024, 128) for p in pieces], axis=1)).astype(BF16)
         for j in range(len(pieces)):
@@ -353,16 +372,13 @@
         elif t < 11:
             RO[t - 2] = tile
 
-    for q in (0, 2):
-        unfold(store_in(q), [G[:, :, :, q, 4], G[:, :, :, q + 1, 4]])
-    unfold(store_direct, [W[:, :, :, 2]])
-
     def fwd(first, count_tiles, main_tiles):
         wm = jnp.concatenate([m.reshape(1024, 128) for m in main_tiles], axis=1)
         wr = jnp.concatenate([RW[first + t] for t in range(count_tiles)], axis=1)
         pre_all = nn_dot(NM[:, :1024], wm) + nn_dot(NM[:, 1024:], wr)
+        bias = BS[:, pl.ds(pl.multiple_of(128 * first, 128), 128 * count_tiles)]
         for t in range(count_tiles):
-            pre = pre_all[:, 128 * t : 128 * t + 128] + bin_ref[first + t]
+            pre = pre_all[:, 128 * t : 128 * t + 128] + bias[:, 128 * t : 128 * t + 128]
             sq = pre * pre
             th = jnp.tanh(GELU_SCALE * pre * (1.0 + GELU_CUBIC * sq))
             half = 0.5 * (1.0 + th)
@@ -376,7 +392,23 @@
             q, half = p // 2, p % 2
             fwd(4 * p, 4, [G[:, :, :, q, 5 * half + t] for t in range(4)])
 
+    y_in(3)
+    for g in range(5):
+        got(("pF", g))
+    got(("pI",))
+    for q in (0, 2):
+        unfold(store_in(q), [G[:, :, :, q, 4], G[:, :, :, q + 1, 4]])
+    unfold(store_direct, [W[:, :, :, 2]])
+
+    y_in(4)
+    for g in range(3):
+        d_partner(g)
+    for i, device in enumerate(plane_devs):
+        same(("t2", i), TB.at[c, v], device)
     fwd(32, 2, [W[:, :, :, 0], W[:, :, :, 1]])
+    for g in range(5):
+        got(("pG", g))
+
     d_in(3, 0)
     fwd_pair(0)
     d_in(3, 1)
@@ -388,18 +420,18 @@
     d_partner(4)
     fwd_pair(6)
 
+    def first_tile(member):
+        return 4 * member + member // 4
+
+    for i, (p, device) in enumerate(zip(ring_peers, ring_devs)):
+        send(("h", i), HS.at[pl.ds(first_tile(p), 5)], HA.at[s], device)
+    HA[s] = HS[pl.ds(first_tile(s), 5)]
+    for i in range(15):
+        got(("t2", i))
+    same(("t3",), TB.at[c], partner)
     for g in range(5):
         got(("pD", g))
     unfold(lambda j, a, tile: store_direct(j, a, tile, 8), [W[:, :, :, 12]])
-    def first_tile(member):
-        return 4 * member + member // 4
-
-    for i in range(15):
-        got(("t2", i))
-    same(("t3",), TB.at[c], partner)
-    for i, (p, device) in enumerate(zip(ring_peers, ring_devs)):
-        send(("h", i), HS.at[pl.ds(first_tile(p), 5)], HA.at[s], device)
-    HA[s] = HS[pl.ds(first_tile(s), 5)]
     for i in range(7):
         got(("h", i))
     last_mine = jnp.where(s % 4 == 3, 1.0, 0.0)
@@ -419,19 +451,19 @@
     for i, (p, device) in enumerate(zip(ring_peers, ring_devs)):
         send(("p", i), PB.at[p], PR.at[s], device)
     PR[s] = PB[s]
+    got(("t3",))
+    texts_nat = jnp.concatenate([TB[0].reshape(256, 640), TB[1].reshape(256, 640)[:, :512]], axis=1)
+    texts = nn_dot(texts_nat, PM[...]).astype(BF16)
     for i in range(7):
         got(("p", i))
     mixed = jnp.sum(PR[...].reshape(8, D), axis=0, keepdims=True)
     pooled = (xsum + mixed) / count + bout
 
-    got(("t3",))
-    texts_nat = jnp.concatenate([TB[0].reshape(256, 640), TB[1].reshape(256, 640)[:, :512]], axis=1)
-    texts = nn_dot(texts_nat, PM[...]).astype(BF16)
     img_norm = jnp.sqrt(jnp.sum(pooled * pooled, axis=1, keepdims=True) + NORM_EPS)
     img_unit = pooled / img_norm
     img_b = img_unit.astype(BF16)
-    scale = jnp.exp(sc_ref[0:1, 0:1])
-    shift = sc_ref[1:2, 0:1]
+    scale = jnp.exp(jnp.zeros((1, 128), F32) + lp_ref[0])[:, 0:1]
+    shift = lp_ref[1]
     def terms(inner, same_label):
         logits = scale * inner + shift
         sign = jnp.where(same_label, 1.0, -1.0)
@@ -441,11 +473,14 @@
 
     img_rows = jnp.broadcast_to(img_b.astype(F32), (16, D)).astype(BF16)
     inner = nt_dot(img_rows, texts)[0:8]
-    img_nat = nt_dot(img_rows, PM[...])[0:1]
-    labels = labl_ref[...]
-    lane256 = lax.broadcasted_iota(jnp.int32, (1, 256), 1)
-    own_label = jnp.sum(jnp.where(lane256 == v * 16 + u, labels, 0.0), axis=1, keepdims=True)
     soft, grad = terms(inner, labels == own_label)
+    d_img = scale * exact_dot(grad, texts, nn_dot)[0:1]
+    d_pooled = (d_img - img_unit * jnp.sum(img_unit * d_img, axis=1, keepdims=True)) / img_norm
+    row_grad = d_pooled / count
+
+    GB[s] = row_grad
+    for i, device in enumerate(ring_devs):
+        same(("g", i), GB.at[s], device)
     stats = [
         jnp.sum(soft[0:1], axis=1, keepdims=True),
         jnp.sum((grad * scale * inner)[0:1], axis=1, keepdims=True),
@@ -453,17 +488,10 @@
     ]
     lane128 = lax.broadcasted_iota(jnp.int32, (1, 128), 1)
     stat_row = sum(jnp.where(lane128 == k, stats[k], 0.0) for k in range(3))
+    img_nat = nt_dot(img_rows, PM[...])[0:1]
     ICOL[u] = jnp.concatenate([img_nat, stat_row], axis=1)
     for i, device in enumerate(col_devs):
         same(("i1", i), ICOL.at[u], device)
-
-    d_img = scale * exact_dot(grad, texts, nn_dot)[0:1]
-    d_pooled = (d_img - img_unit * jnp.sum(img_unit * d_img, axis=1, keepdims=True)) / img_norm
-    row_grad = d_pooled / count
-
-    GB[s] = row_grad
-    for i, device in enumerate(ring_devs):
-        same(("g", i), GB.at[s], device)
     for i in range(7):
         got(("g", i))
     grads = GB[...].reshape(8, D).astype(BF16)
@@ -485,13 +513,6 @@
         lax.broadcasted_iota(jnp.int32, (16, 256), 1) == 16 * lax.broadcasted_iota(jnp.int32, (16, 256), 0) + u
     )
     texts16 = nn_dot(jnp.where(pick, 1.0, 0.0).astype(BF16), texts_nat).astype(BF16)
-    lab2 = lab2_ref[...]
-    lab_txt = jnp.sum(
-        jnp.where(lax.broadcasted_iota(jnp.int32, (16, 128), 1) == u, lab2, 0.0), axis=1, keepdims=True
-    )
-    lab_img = jnp.sum(
-        jnp.where(lax.broadcasted_iota(jnp.int32, (16, 128), 0) == v, lab2, 0.0), axis=0, keepdims=True
-    )[:, :16]
     _, grad_t = terms(nt_dot(texts16, imgs), lab_txt == lab_img)
     d_part = exact_dot(grad_t, imgs, nn_dot)
     col_stats = jnp.sum(column[:, D:], axis=0, keepdims=True)
@@ -546,11 +567,12 @@
     for i in range(15):
         got(("i2", i))
     sums = jnp.sum(DT[...].reshape(16, 1280), axis=0, keepdims=True)
-    st_ref[...] = sums[:, D:] / 256.0
+    for k in range(3):
+        st_ref[k] = jnp.sum(jnp.where(lane128 == k, sums[:, D:], 0.0)) / 256.0
     d_txt = scale * sums[:, :D]
     unit = TROW[...]
     tg = (d_txt - unit * jnp.sum(unit * d_txt, axis=1, keepdims=True)) / jnp.sqrt(
-        jnp.sum(vec_ref[3:4, :] * vec_ref[3:4, :], axis=1, keepdims=True) + NORM_EPS
+        jnp.sum(VEC[3:4, :] * VEC[3:4, :], axis=1, keepdims=True) + NORM_EPS
     )
     tg_ref[...] = tg.astype(BF16)
 
@@ -562,17 +584,6 @@
     patches, counts, norm_gain, norm_bias, weight_in, bias_in, weight_out, bias_out, text_embed, pair_label,
     logit_params,
 ):
-    rows = patches.reshape(ROWS, D)
-    wi = jnp.pad(weight_in, ((0, 12), (0, 48)))
-    wo = jnp.pad(weight_out, ((0, 48), (0, 0)))
-    vec = jnp.concatenate(
-        [norm_gain[None], norm_bias[None], bias_out[None], text_embed.astype(F32), jnp.zeros((4, D), F32)], axis=0
-    )
-    bias = jnp.pad(bias_in, (0, 48)).reshape(NT_IN, 1, 128)
-    labels = jnp.transpose(pair_label.reshape(2, 8, 2, 4, 2), (3, 0, 4, 1, 2)).reshape(16, 16).astype(F32)
-    scal = jnp.broadcast_to(
-        jnp.concatenate([logit_params, counts.reshape(1).astype(F32), jnp.zeros((5,), F32)])[:, None], (8, 128)
-    )
     vm = pltpu.VMEM
     scratch = [
         vm((2, 8, 2, 4, 9, 32, 128), BF16),
@@ -602,25 +613,33 @@
         vm((16, 1, 1280), F32),
         vm((16, 1, 1280), F32),
         vm((16, 1, 1280), F32),
+        vm((2, 48, 4352), BF16),
+        vm((1, 4352), F32),
+        vm((8, D), F32),
         pltpu.SemaphoreType.DMA((N_COPIES,)),
         pltpu.SemaphoreType.DMA((N_COPIES,)),
     ]
     spec = pl.BlockSpec(memory_space=pltpu.VMEM)
+    smem = pl.BlockSpec(memory_space=pltpu.SMEM)
     patch_grad, text_grad, stats = pl.pallas_call(
         kernel,
         out_shape=(
             jax.ShapeDtypeStruct((ROWS, D), BF16),
             jax.ShapeDtypeStruct((1, D), BF16),
-            jax.ShapeDtypeStruct((1, 128), F32),
+            jax.ShapeDtypeStruct((3,), F32),
         ),
-        in_specs=[spec] * 8,
-        out_specs=(spec, spec, spec),
+        in_specs=[spec] * 6 + [smem] * 2,
+        out_specs=(spec, spec, smem),
         scratch_shapes=scratch,
         compiler_params=pltpu.CompilerParams(
             collective_id=0, has_side_effects=True, vmem_limit_bytes=56 * 2**20
         ),
-    )(rows, wi, wo, vec, bias, labels.reshape(1, 256), jnp.pad(labels, ((0, 0), (0, 112))), scal)
-    return patch_grad.reshape(patches.shape), text_grad, stats[0, :3]
+    )(
+        patches.reshape(ROWS, D), weight_in, weight_out.T,
+        jnp.concatenate([norm_gain, norm_bias, bias_out, bias_in]).reshape(1, 3 * D + FF),
+        text_embed, pair_label.reshape(1, 256), logit_params, counts.reshape(1),
+    )
+    return patch_grad.reshape(patches.shape), text_grad, stats
 
 
 def solution(mesh):

time: 104 us -> 93.7 us (0.901)
  local copies, waits for them, and re-layouts: 11.3 us -> 3.77 us
  Pallas kernels: 90.2 us -> 87.7 us
    pad x4 -> x0, local copies, waits for them, and re-layouts: 2.61 us -> none  [the longest x1 1.22 us: shards(): wo = jnp.pad(weight_out, ((0, 48), (0, 0)))]
    pallas_call x1, Pallas kernels: 90.2 us -> 87.7 us  [shards(): pl.pallas_call(kernel, out_shape=(jax.ShapeDtypeStruct((ROWS, D), BF16),...]
    convert_element_type x4 -> x0, local copies, waits for them, and re-layouts: 1.47 us -> none  [shards(): jnp.transpose(pair_label.reshape(2, 8, 2, 4, 2), (3, 0, 4, 1, 2))]
    squeeze x1 -> x0, local copies, waits for them, and re-layouts: 1.18 us -> none  [shards(): return (patch_grad.reshape(patches.shape), text_grad, stats[0, :3])]
    unnamed x19 -> x9, local copies, waits for them, and re-layouts: 4.07 us -> 3.13 us
where the time goes in v3:
time: 93.7 us; the launch traced here: 93.5 us
  Pallas kernels  87.7 us (94%)
  local copies, waits for them, and re-layouts  3.77 us (4%)
  between operations  1.32 us (1%)
    pallas_call x1, Pallas kernels, shards(): pl.pallas_call(kernel, out_shape=(jax.ShapeDtypeStruct((ROWS, D), BF16),...  87.7 us
    unnamed x9, local copies, waits for them, and re-layouts  3.13 us

profile of v3, /device:TPU:1, one launch (start us, length us, event | category | flops | bytes accessed | tf_op | source)
XLA Modules:
  0.0 93.5 jit_solution(7230084456544494338)
XLA Ops:
  0.6 0.0 copy-start
  1.3 0.0 copy-done
  1.3 0.7 pad_maximum_fusion
  2.1 0.6 reshape.22.vec_in
  2.7 87.7 %shard_map.130 = (bf16[256,1152]{1,0:T(8,128)(2,1)}, bf16[1,1152]{1,0:T(2,128)(2,1)}, f32[3]{0:T(128)}) custom-call(bf16[256,1152]{1,0:T(8,128)(2,1)} %bitcast.6, bf16[36,4304]{1,0:T(8,128)(2,1)} %wi_in.1, bf16[36,4304]{1,0:T(8,128)(2,1)} %bitcast.8, f32[1,7760]{1,0:T(1,128)} %reshape.22.vec_in, bf16[1,1152]{1,0:T(2,128)(2,1)} %text_in.1, s32[1,256]{1,0:T(1,128)} %bitcast.9, ...), custom_call_target="tpu_custom_call" | custom-call | tf_op jit(solution)/shard_map/pallas_call | solution.py:624
  90.4 0.0 copy-start.1
  90.4 1.9 %copy.18 = bf16[1,1,256,1152]{3,2,1,0:T(8,128)(2,1)} copy(bf16[1,1,256,1152]{3,2,1,0:T(8,128)(2,1)} %bitcast.7) | data formatting | bytes 1179648
  92.3 0.0 copy-done.1
  92.3 0.0 copy-start.2
  92.3 0.6 copy.19
  92.9 0.1 copy-done.2
  93.0 0.5 copy.20
Async XLA Ops:
  0.6 0.7 copy-start
  90.4 1.9 %copy-start.1 = (bf16[1,1152]{1,0:T(2,128)(2,1)S(1)}, bf16[1,1152]{1,0:T(2,128)(2,1)}, u32[]{:S(2)}) copy-start(bf16[1,1152]{1,0:T(2,128)(2,1)} %get-tuple-element.13) | copy-start | bytes 6916
  92.3 0.7 copy-start.2

commit v4 on v3

--- a/solution.py
+++ b/solution.py
@@ -409,16 +409,16 @@
     for g in range(5):
         got(("pG", g))
 
+    fwd_pair(0)
     d_in(3, 0)
-    fwd_pair(0)
     d_in(3, 1)
+    fwd_pair(2)
     d_partner(3)
-    fwd_pair(2)
+    fwd_pair(4)
+    fwd_pair(6)
     d_in(4, 0)
-    fwd_pair(4)
     d_in(4, 1)
     d_partner(4)
-    fwd_pair(6)
 
     def first_tile(member):
         return 4 * member + member // 4

time: 93.7 us -> 92.7 us (0.989)
  Pallas kernels: 87.7 us -> 86.6 us
    pallas_call x1, Pallas kernels: 87.7 us -> 86.6 us  [shards(): pl.pallas_call(kernel, out_shape=(jax.ShapeDtypeStruct((ROWS, D), BF16),...]
where the time goes in v4:
time: 92.7 us; the launch traced here: 92.4 us
  Pallas kernels  86.6 us (93%)
  local copies, waits for them, and re-layouts  3.77 us (4%)
  between operations  1.32 us (1%)
    pallas_call x1, Pallas kernels, shards(): pl.pallas_call(kernel, out_shape=(jax.ShapeDtypeStruct((ROWS, D), BF16),...  86.6 us
    unnamed x9, local copies, waits for them, and re-layouts  3.13 us

profile of v4, /device:TPU:1, one launch (start us, length us, event | category | flops | bytes accessed | tf_op | source)
XLA Modules:
  0.0 92.4 jit_solution(1139320649137463398)
XLA Ops:
  0.6 0.0 copy-start
  1.3 0.0 copy-done
  1.3 0.7 pad_maximum_fusion
  2.1 0.6 reshape.22.vec_in
  2.7 86.6 %shard_map.130 = (bf16[256,1152]{1,0:T(8,128)(2,1)}, bf16[1,1152]{1,0:T(2,128)(2,1)}, f32[3]{0:T(128)}) custom-call(bf16[256,1152]{1,0:T(8,128)(2,1)} %bitcast.6, bf16[36,4304]{1,0:T(8,128)(2,1)} %wi_in.1, bf16[36,4304]{1,0:T(8,128)(2,1)} %bitcast.8, f32[1,7760]{1,0:T(1,128)} %reshape.22.vec_in, bf16[1,1152]{1,0:T(2,128)(2,1)} %text_in.1, s32[1,256]{1,0:T(1,128)} %bitcast.9, ...), custom_call_target="tpu_custom_call" | custom-call | tf_op jit(solution)/shard_map/pallas_call | solution.py:624
  89.3 0.0 copy-start.1
  89.3 1.9 %copy.18 = bf16[1,1,256,1152]{3,2,1,0:T(8,128)(2,1)} copy(bf16[1,1,256,1152]{3,2,1,0:T(8,128)(2,1)} %bitcast.7) | data formatting | bytes 1179648
  91.3 0.0 copy-done.1
  91.3 0.0 copy-start.2
  91.3 0.6 copy.19
  91.9 0.1 copy-done.2
  91.9 0.5 copy.20
Async XLA Ops:
  0.6 0.7 copy-start
  89.3 1.9 %copy-start.1 = (bf16[1,1152]{1,0:T(2,128)(2,1)S(1)}, bf16[1,1152]{1,0:T(2,128)(2,1)}, u32[]{:S(2)}) copy-start(bf16[1,1152]{1,0:T(2,128)(2,1)} %get-tuple-element.13) | copy-start | bytes 6916
  91.3 0.7 copy-start.2
